TPU v7x, 512 devices: a whole 4x8x8 slice. The times are simulated.
512 devices in a mesh: ctx: 64 (over z, y), head: 2 (over core), dp: 4 (over x).
Axes of the slice: x: 4, y: 8, z: 8, core: 2. Of those that a mesh axis runs over, the one named last changes fastest.
Arguments:
- query: bfloat16 [65536, 2048], P(('dp', 'ctx'), 'head'), parts along dimension 0, may hold values from -6 to 6
- keys: bfloat16 [65536, 512], P(('dp', 'ctx'), 'head'), parts along dimension 0, may hold values from -6 to 6
- values: bfloat16 [65536, 512], P(('dp', 'ctx'), 'head'), parts along dimension 0, may hold values from -6 to 6
- output: bfloat16 [65536, 2048], P(('dp', 'ctx'), 'head'), parts along dimension 0, may hold values from -1.5 to 1.5
- output_gradient: bfloat16 [65536, 2048], P(('dp', 'ctx'), 'head'), parts along dimension 0, may hold values from -48 to 48
- row_log_norm: float32 [16, 65536], P('head', ('dp', 'ctx')), parts along dimension 1, may hold values from 4 to 7
- doc_lengths: int32 [64], P('dp'), parts along dimension 0, may hold values from 1 to 2048, as said below
Outputs:
- grad_query: bfloat16 [65536, 2048], P(('dp', 'ctx'), 'head'), parts along dimension 0
- key_gradient: bfloat16 [65536, 512], P(('dp', 'ctx'), 'head'), parts along dimension 0
- value_gradient: bfloat16 [65536, 512], P(('dp', 'ctx'), 'head'), parts along dimension 0
There are 4 independent parts, one for each index of `dp`. A program takes and returns all parts, laid end to end along the dimension named above; each array names one. Nothing has to cross between parts.
Inputs may be any that keep to these rules, and one draw needn't show every extreme that they name: `doc_lengths`: the 16 documents fill the 16384 positions in order; one of them, at any place, holds exactly 2048 tokens.
All inputs are finite; a program needn't handle non-finite values.
Results may differ from a plain program's by a relative error of at most 0.013.
Values may be sent and summed in bfloat16 or wider, within the bound.
No kernel may reach another device: no remote copies, remote signals or barrier semaphores. Data moves between devices by JAX's collectives and lax.ppermute only.
A program may use at most 128 MiB of HBM per device.

v0:
```python
import jax
import jax.numpy as jnp
from jax import lax
from jax.sharding import PartitionSpec as P

HEAD_WIDTH = 128


def passed_along(value, axis, steps):
    count = lax.axis_size(axis)
    first, last = (max(0, -steps), min(count, count - steps))
    return lax.ppermute(value, axis, [(source, source + steps) for source in range(first, last)])


def shifted(array, axis, by):
    length = lax.axis_size(axis)
    return lax.ppermute(array, axis, [(i, (i + by) % length) for i in range(length)])


def locate_docs(positions, doc_ends):
    return jnp.sum((doc_ends[None, :] <= positions[:, None]).astype(jnp.int32), axis=1)


def tile_terms(
    query_rows,
    output_gradient_rows,
    lse,
    delta_rows,
    q_docs,
    q_pos,
    key_block_slice,
    value_block_slice,
    k_pos,
    doc_ends,
    softmax_scale,
):
    k_docs = locate_docs(k_pos, doc_ends)
    live = (
        (k_docs[None, :] == q_docs[:, None])
        & (k_pos[None, :] <= q_pos[:, None])
        & (k_pos[None, :] >= 0)
    )
    score_matrix = (
        jnp.einsum(
            "wmax,pmx->mawp", query_rows, key_block_slice, preferred_element_type=jnp.float32
        )
        * softmax_scale
    )
    prob = jnp.where(live[None, None], jnp.exp(score_matrix - lse[..., None]), 0.0)
    probability_gradient = jnp.einsum(
        "wmax,pmx->mawp",
        output_gradient_rows,
        value_block_slice,
        preferred_element_type=jnp.float32,
    )
    score_gradient = (prob * (probability_gradient - delta_rows[..., None])).astype(jnp.bfloat16)
    probability_block = prob.astype(jnp.bfloat16)
    value_gradient_piece = jnp.einsum(
        "vfiy,ivfq->yvq",
        probability_block,
        output_gradient_rows,
        preferred_element_type=jnp.float32,
    )
    key_gradient_piece = jnp.einsum(
        "vfiy,ivfq->yvq", score_gradient, query_rows, preferred_element_type=jnp.float32
    )
    query_gradient_piece = jnp.einsum(
        "vyxz,zvh->xvyh", score_gradient, key_block_slice, preferred_element_type=jnp.float32
    )
    return (query_gradient_piece, key_gradient_piece, value_gradient_piece)


def body(query, keys, values, output, output_gradient, row_log_norm, doc_lengths):
    rows = query.shape[0]
    groups = keys.shape[1] // HEAD_WIDTH
    per_group = query.shape[1] // (groups * HEAD_WIDTH)
    softmax_scale = HEAD_WIDTH ** (-0.5)
    index = lax.axis_index("ctx")
    span = min(8, lax.axis_size("ctx") // 2)
    local = jnp.arange(rows, dtype=jnp.int32)
    q_pos = index * rows + local
    doc_ends = jnp.cumsum(doc_lengths)
    q_docs = locate_docs(q_pos, doc_ends)
    query_rows = query.reshape(rows, groups, per_group, HEAD_WIDTH)
    output_gradient_rows = output_gradient.reshape(rows, groups, per_group, HEAD_WIDTH)
    output_rows = output.reshape(rows, groups, per_group, HEAD_WIDTH)
    k_own = keys.reshape(rows, groups, HEAD_WIDTH)
    v_own = values.reshape(rows, groups, HEAD_WIDTH)
    lse = row_log_norm.reshape(groups, per_group, rows)
    delta_rows = jnp.einsum(
        "wokc,wokc->okw", output_gradient_rows, output_rows, preferred_element_type=jnp.float32
    )

    def terms(key_block_slice, value_block_slice, k_pos):
        return tile_terms(
            query_rows,
            output_gradient_rows,
            lse,
            delta_rows,
            q_docs,
            q_pos,
            key_block_slice,
            value_block_slice,
            k_pos,
            doc_ends,
            softmax_scale,
        )

    dq_first, dk_first, dv_first = terms(k_own, v_own, q_pos)

    def advance(turn, carry):
        k_cur, v_cur, dk_acc, dv_acc, dq_acc = carry
        k_cur, v_cur = passed_along((k_cur, v_cur), "ctx", 1)
        dk_acc, dv_acc = shifted((dk_acc, dv_acc), "ctx", 1)
        k_pos = (index - turn) * rows + local
        query_gradient_piece, key_gradient_piece, value_gradient_piece = terms(k_cur, v_cur, k_pos)
        return (
            k_cur,
            v_cur,
            dk_acc + key_gradient_piece,
            dv_acc + value_gradient_piece,
            dq_acc + query_gradient_piece,
        )

    finals = lax.fori_loop(1, span + 1, advance, (k_own, v_own, dk_first, dv_first, dq_first))
    dq_total = finals[4]
    dk_home, dv_home = (
        shifted(finals[2].astype(jnp.bfloat16), "ctx", -span).astype(jnp.float32),
        shifted(finals[3].astype(jnp.bfloat16), "ctx", -span).astype(jnp.float32),
    )
    grad_query = (softmax_scale * dq_total).reshape(rows, -1).astype(jnp.bfloat16)
    key_gradient = (softmax_scale * dk_home).reshape(rows, -1).astype(jnp.bfloat16)
    value_gradient = dv_home.reshape(rows, -1).astype(jnp.bfloat16)
    return (grad_query, key_gradient, value_gradient)


def solution(mesh):
    in_specs = (
        P(("dp", "ctx"), "head"),
        P(("dp", "ctx"), "head"),
        P(("dp", "ctx"), "head"),
        P(("dp", "ctx"), "head"),
        P(("dp", "ctx"), "head"),
        P("head", ("dp", "ctx")),
        P("dp"),
    )
    out_specs = (P(("dp", "ctx"), "head"), P(("dp", "ctx"), "head"), P(("dp", "ctx"), "head"))
    return jax.shard_map(body, mesh=mesh, in_specs=in_specs, out_specs=out_specs, check_vma=False)
```

profile of v0, /device:TPU:198, one launch (start us, length us, event | category | flops | bytes accessed | tf_op | source)
XLA Modules:
  0.0 221.7 jit_solution(9864192958514727605)
XLA Ops:
  16.7 184.4 %while.23 = (s32[]{:T(128)}, bf16[256,2,128]{2,0,1:T(8,128)(2,1)S(1)}, bf16[256,2,128]{2,0,1:T(8,128)(2,1)S(1)}, f32[256,2,128]{2,0,1:T(8,128)S(1)}, f32[256,2,1...) while((s32[]{:T(128)}, ...), condition=%wide.wide.region_4.5_spmd.clone, body=%wide.wide.region_2.4_spmd.clone.sunk | while | flops 675427072 | bytes 18899872 | solution.py:125
  16.7 3.5 %collective-permute-start.1 = (bf16[256,2,128]{2,0,1:T(8,128)(2,1)S(1)}, bf16[256,2,128]{2,0,1:T(8,128)(2,1)S(1)}, u32[]{:S(2)}, u32[]{:S(2)}) collective-permute-start(bf16[256,2,128]{2,0,1:T(8,128)(2,1)S(1)} %get-tuple-element.506), channel_id=1, source_target_pairs={{0,8},{8,16},{16,24},{24,32},{32,40},{40,48},{48,56},{56,64},{64,7... | collective-permute-start | bytes 393224 | tf_op jit(solution)/shard_map/while/body/eval_jaxpr/ppermute | solution.py:12
  20.2 3.5 %collective-permute-start = (bf16[256,2,128]{2,0,1:T(8,128)(2,1)S(1)}, bf16[256,2,128]{2,0,1:T(8,128)(2,1)S(1)}, u32[]{:S(2)}, u32[]{:S(2)}) collective-permute-start(bf16[256,2,128]{2,0,1:T(8,128)(2,1)S(1)} %get-tuple-element.505), channel_id=1, source_target_pairs={{0,8},{8,16},{16,24},{24,32},{32,40},{40,48},{48,56},{56,64},{64,7... | collective-permute-start | bytes 393224 | tf_op jit(solution)/shard_map/while/body/eval_jaxpr/ppermute | solution.py:12
  23.7 3.5 %collective-permute-start.3 = (f32[256,2,128]{2,0,1:T(8,128)}, f32[256,2,128]{2,0,1:T(8,128)S(1)}, u32[]{:S(2)}, u32[]{:S(2)}) collective-permute-start(f32[256,2,128]{2,0,1:T(8,128)} %get-tuple-element.508), channel_id=1, source_target_pairs={{0,8},{8,16},{16,24},{24,32},{32,40},{40,48},{48,56},{56,64},{64,7... | collective-permute-start | bytes 786440 | tf_op jit(solution)/shard_map/while/body/eval_jaxpr/ppermute | solution.py:17
  27.2 4.7 %collective-permute-start.2 = (f32[256,2,128]{2,0,1:T(8,128)S(1)}, f32[256,2,128]{2,0,1:T(8,128)S(1)}, u32[]{:S(2)}, u32[]{:S(2)}) collective-permute-start(f32[256,2,128]{2,0,1:T(8,128)S(1)} %get-tuple-element.507), channel_id=1, source_target_pairs={{0,8},{8,16},{16,24},{24,32},{32,40},{40,48},{48,56},{56,64},{64,7... | collective-permute-start | bytes 786440 | tf_op jit(solution)/shard_map/while/body/eval_jaxpr/ppermute | solution.py:17
  38.3 2.7 %collective-permute-done.2 = f32[256,2,128]{2,0,1:T(8,128)S(1)} collective-permute-done((f32[256,2,128]{2,0,1:T(8,128)S(1)}, f32[256,2,128]{2,0,1:T(8,128)S(1)}, u32[]{:S(2)}, u32[]{:S(2)}) %collective-permute-start.2) | collective-permute-done | bytes 262176 | tf_op jit(solution)/shard_map/while/body/eval_jaxpr/ppermute | solution.py:17
  43.4 4.1 %collective-permute-start = (bf16[256,2,128]{2,0,1:T(8,128)(2,1)S(1)}, bf16[256,2,128]{2,0,1:T(8,128)(2,1)S(1)}, u32[]{:S(2)}, u32[]{:S(2)}) collective-permute-start(bf16[256,2,128]{2,0,1:T(8,128)(2,1)S(1)} %get-tuple-element.505), channel_id=1, source_target_pairs={{0,8},{8,16},{16,24},{24,32},{32,40},{40,48},{48,56},{56,64},{64,7... | collective-permute-start | bytes 393224 | tf_op jit(solution)/shard_map/while/body/eval_jaxpr/ppermute | solution.py:12
  47.5 2.9 %collective-permute-start.3 = (f32[256,2,128]{2,0,1:T(8,128)}, f32[256,2,128]{2,0,1:T(8,128)S(1)}, u32[]{:S(2)}, u32[]{:S(2)}) collective-permute-start(f32[256,2,128]{2,0,1:T(8,128)} %get-tuple-element.508), channel_id=1, source_target_pairs={{0,8},{8,16},{16,24},{24,32},{32,40},{40,48},{48,56},{56,64},{64,7... | collective-permute-start | bytes 786440 | tf_op jit(solution)/shard_map/while/body/eval_jaxpr/ppermute | solution.py:17
  50.4 4.3 %collective-permute-start.2 = (f32[256,2,128]{2,0,1:T(8,128)S(1)}, f32[256,2,128]{2,0,1:T(8,128)S(1)}, u32[]{:S(2)}, u32[]{:S(2)}) collective-permute-start(f32[256,2,128]{2,0,1:T(8,128)S(1)} %get-tuple-element.507), channel_id=1, source_target_pairs={{0,8},{8,16},{16,24},{24,32},{32,40},{40,48},{48,56},{56,64},{64,7... | collective-permute-start | bytes 786440 | tf_op jit(solution)/shard_map/while/body/eval_jaxpr/ppermute | solution.py:17
  57.5 3.4 %collective-permute-done.3 = f32[256,2,128]{2,0,1:T(8,128)S(1)} collective-permute-done((f32[256,2,128]{2,0,1:T(8,128)}, f32[256,2,128]{2,0,1:T(8,128)S(1)}, u32[]{:S(2)}, u32[]{:S(2)}) %collective-permute-start.3) | collective-permute-done | bytes 262176 | tf_op jit(solution)/shard_map/while/body/eval_jaxpr/ppermute | solution.py:17
  66.1 3.5 %collective-permute-start = (bf16[256,2,128]{2,0,1:T(8,128)(2,1)S(1)}, bf16[256,2,128]{2,0,1:T(8,128)(2,1)S(1)}, u32[]{:S(2)}, u32[]{:S(2)}) collective-permute-start(bf16[256,2,128]{2,0,1:T(8,128)(2,1)S(1)} %get-tuple-element.505), channel_id=1, source_target_pairs={{0,8},{8,16},{16,24},{24,32},{32,40},{40,48},{48,56},{56,64},{64,7... | collective-permute-start | bytes 393224 | tf_op jit(solution)/shard_map/while/body/eval_jaxpr/ppermute | solution.py:12
  69.6 3.6 %collective-permute-start.3 = (f32[256,2,128]{2,0,1:T(8,128)}, f32[256,2,128]{2,0,1:T(8,128)S(1)}, u32[]{:S(2)}, u32[]{:S(2)}) collective-permute-start(f32[256,2,128]{2,0,1:T(8,128)} %get-tuple-element.508), channel_id=1, source_target_pairs={{0,8},{8,16},{16,24},{24,32},{32,40},{40,48},{48,56},{56,64},{64,7... | collective-permute-start | bytes 786440 | tf_op jit(solution)/shard_map/while/body/eval_jaxpr/ppermute | solution.py:17
  73.2 4.0 %collective-permute-start.2 = (f32[256,2,128]{2,0,1:T(8,128)S(1)}, f32[256,2,128]{2,0,1:T(8,128)S(1)}, u32[]{:S(2)}, u32[]{:S(2)}) collective-permute-start(f32[256,2,128]{2,0,1:T(8,128)S(1)} %get-tuple-element.507), channel_id=1, source_target_pairs={{0,8},{8,16},{16,24},{24,32},{32,40},{40,48},{48,56},{56,64},{64,7... | collective-permute-start | bytes 786440 | tf_op jit(solution)/shard_map/while/body/eval_jaxpr/ppermute | solution.py:17
  80.1 3.0 %collective-permute-done.3 = f32[256,2,128]{2,0,1:T(8,128)S(1)} collective-permute-done((f32[256,2,128]{2,0,1:T(8,128)}, f32[256,2,128]{2,0,1:T(8,128)S(1)}, u32[]{:S(2)}, u32[]{:S(2)}) %collective-permute-start.3) | collective-permute-done | bytes 262176 | tf_op jit(solution)/shard_map/while/body/eval_jaxpr/ppermute | solution.py:17
  88.7 3.1 %collective-permute-start = (bf16[256,2,128]{2,0,1:T(8,128)(2,1)S(1)}, bf16[256,2,128]{2,0,1:T(8,128)(2,1)S(1)}, u32[]{:S(2)}, u32[]{:S(2)}) collective-permute-start(bf16[256,2,128]{2,0,1:T(8,128)(2,1)S(1)} %get-tuple-element.505), channel_id=1, source_target_pairs={{0,8},{8,16},{16,24},{24,32},{32,40},{40,48},{48,56},{56,64},{64,7... | collective-permute-start | bytes 393224 | tf_op jit(solution)/shard_map/while/body/eval_jaxpr/ppermute | solution.py:12
  91.8 3.6 %collective-permute-start.3 = (f32[256,2,128]{2,0,1:T(8,128)}, f32[256,2,128]{2,0,1:T(8,128)S(1)}, u32[]{:S(2)}, u32[]{:S(2)}) collective-permute-start(f32[256,2,128]{2,0,1:T(8,128)} %get-tuple-element.508), channel_id=1, source_target_pairs={{0,8},{8,16},{16,24},{24,32},{32,40},{40,48},{48,56},{56,64},{64,7... | collective-permute-start | bytes 786440 | tf_op jit(solution)/shard_map/while/body/eval_jaxpr/ppermute | solution.py:17
  95.5 4.3 %collective-permute-start.2 = (f32[256,2,128]{2,0,1:T(8,128)S(1)}, f32[256,2,128]{2,0,1:T(8,128)S(1)}, u32[]{:S(2)}, u32[]{:S(2)}) collective-permute-start(f32[256,2,128]{2,0,1:T(8,128)S(1)} %get-tuple-element.507), channel_id=1, source_target_pairs={{0,8},{8,16},{16,24},{24,32},{32,40},{40,48},{48,56},{56,64},{64,7... | collective-permute-start | bytes 786440 | tf_op jit(solution)/shard_map/while/body/eval_jaxpr/ppermute | solution.py:17
  110.9 3.3 %collective-permute-start = (bf16[256,2,128]{2,0,1:T(8,128)(2,1)S(1)}, bf16[256,2,128]{2,0,1:T(8,128)(2,1)S(1)}, u32[]{:S(2)}, u32[]{:S(2)}) collective-permute-start(bf16[256,2,128]{2,0,1:T(8,128)(2,1)S(1)} %get-tuple-element.505), channel_id=1, source_target_pairs={{0,8},{8,16},{16,24},{24,32},{32,40},{40,48},{48,56},{56,64},{64,7... | collective-permute-start | bytes 393224 | tf_op jit(solution)/shard_map/while/body/eval_jaxpr/ppermute | solution.py:12
  114.2 4.4 %collective-permute-start.3 = (f32[256,2,128]{2,0,1:T(8,128)}, f32[256,2,128]{2,0,1:T(8,128)S(1)}, u32[]{:S(2)}, u32[]{:S(2)}) collective-permute-start(f32[256,2,128]{2,0,1:T(8,128)} %get-tuple-element.508), channel_id=1, source_target_pairs={{0,8},{8,16},{16,24},{24,32},{32,40},{40,48},{48,56},{56,64},{64,7... | collective-permute-start | bytes 786440 | tf_op jit(solution)/shard_map/while/body/eval_jaxpr/ppermute | solution.py:17
  118.6 5.6 %collective-permute-start.2 = (f32[256,2,128]{2,0,1:T(8,128)S(1)}, f32[256,2,128]{2,0,1:T(8,128)S(1)}, u32[]{:S(2)}, u32[]{:S(2)}) collective-permute-start(f32[256,2,128]{2,0,1:T(8,128)S(1)} %get-tuple-element.507), channel_id=1, source_target_pairs={{0,8},{8,16},{16,24},{24,32},{32,40},{40,48},{48,56},{56,64},{64,7... | collective-permute-start | bytes 786440 | tf_op jit(solution)/shard_map/while/body/eval_jaxpr/ppermute | solution.py:17
  133.1 4.7 %collective-permute-start = (bf16[256,2,128]{2,0,1:T(8,128)(2,1)S(1)}, bf16[256,2,128]{2,0,1:T(8,128)(2,1)S(1)}, u32[]{:S(2)}, u32[]{:S(2)}) collective-permute-start(bf16[256,2,128]{2,0,1:T(8,128)(2,1)S(1)} %get-tuple-element.505), channel_id=1, source_target_pairs={{0,8},{8,16},{16,24},{24,32},{32,40},{40,48},{48,56},{56,64},{64,7... | collective-permute-start | bytes 393224 | tf_op jit(solution)/shard_map/while/body/eval_jaxpr/ppermute | solution.py:12
  137.8 4.5 %collective-permute-start.3 = (f32[256,2,128]{2,0,1:T(8,128)}, f32[256,2,128]{2,0,1:T(8,128)S(1)}, u32[]{:S(2)}, u32[]{:S(2)}) collective-permute-start(f32[256,2,128]{2,0,1:T(8,128)} %get-tuple-element.508), channel_id=1, source_target_pairs={{0,8},{8,16},{16,24},{24,32},{32,40},{40,48},{48,56},{56,64},{64,7... | collective-permute-start | bytes 786440 | tf_op jit(solution)/shard_map/while/body/eval_jaxpr/ppermute | solution.py:17
  142.3 5.6 %collective-permute-start.2 = (f32[256,2,128]{2,0,1:T(8,128)S(1)}, f32[256,2,128]{2,0,1:T(8,128)S(1)}, u32[]{:S(2)}, u32[]{:S(2)}) collective-permute-start(f32[256,2,128]{2,0,1:T(8,128)S(1)} %get-tuple-element.507), channel_id=1, source_target_pairs={{0,8},{8,16},{16,24},{24,32},{32,40},{40,48},{48,56},{56,64},{64,7... | collective-permute-start | bytes 786440 | tf_op jit(solution)/shard_map/while/body/eval_jaxpr/ppermute | solution.py:17
  153.8 3.1 %collective-permute-start.1 = (bf16[256,2,128]{2,0,1:T(8,128)(2,1)S(1)}, bf16[256,2,128]{2,0,1:T(8,128)(2,1)S(1)}, u32[]{:S(2)}, u32[]{:S(2)}) collective-permute-start(bf16[256,2,128]{2,0,1:T(8,128)(2,1)S(1)} %get-tuple-element.506), channel_id=1, source_target_pairs={{0,8},{8,16},{16,24},{24,32},{32,40},{40,48},{48,56},{56,64},{64,7... | collective-permute-start | bytes 393224 | tf_op jit(solution)/shard_map/while/body/eval_jaxpr/ppermute | solution.py:12
  156.9 4.5 %collective-permute-start = (bf16[256,2,128]{2,0,1:T(8,128)(2,1)S(1)}, bf16[256,2,128]{2,0,1:T(8,128)(2,1)S(1)}, u32[]{:S(2)}, u32[]{:S(2)}) collective-permute-start(bf16[256,2,128]{2,0,1:T(8,128)(2,1)S(1)} %get-tuple-element.505), channel_id=1, source_target_pairs={{0,8},{8,16},{16,24},{24,32},{32,40},{40,48},{48,56},{56,64},{64,7... | collective-permute-start | bytes 393224 | tf_op jit(solution)/shard_map/while/body/eval_jaxpr/ppermute | solution.py:12
  161.3 4.7 %collective-permute-start.3 = (f32[256,2,128]{2,0,1:T(8,128)}, f32[256,2,128]{2,0,1:T(8,128)S(1)}, u32[]{:S(2)}, u32[]{:S(2)}) collective-permute-start(f32[256,2,128]{2,0,1:T(8,128)} %get-tuple-element.508), channel_id=1, source_target_pairs={{0,8},{8,16},{16,24},{24,32},{32,40},{40,48},{48,56},{56,64},{64,7... | collective-permute-start | bytes 786440 | tf_op jit(solution)/shard_map/while/body/eval_jaxpr/ppermute | solution.py:17
  166.0 5.6 %collective-permute-start.2 = (f32[256,2,128]{2,0,1:T(8,128)S(1)}, f32[256,2,128]{2,0,1:T(8,128)S(1)}, u32[]{:S(2)}, u32[]{:S(2)}) collective-permute-start(f32[256,2,128]{2,0,1:T(8,128)S(1)} %get-tuple-element.507), channel_id=1, source_target_pairs={{0,8},{8,16},{16,24},{24,32},{32,40},{40,48},{48,56},{56,64},{64,7... | collective-permute-start | bytes 786440 | tf_op jit(solution)/shard_map/while/body/eval_jaxpr/ppermute | solution.py:17
  177.5 3.1 %collective-permute-start.1 = (bf16[256,2,128]{2,0,1:T(8,128)(2,1)S(1)}, bf16[256,2,128]{2,0,1:T(8,128)(2,1)S(1)}, u32[]{:S(2)}, u32[]{:S(2)}) collective-permute-start(bf16[256,2,128]{2,0,1:T(8,128)(2,1)S(1)} %get-tuple-element.506), channel_id=1, source_target_pairs={{0,8},{8,16},{16,24},{24,32},{32,40},{40,48},{48,56},{56,64},{64,7... | collective-permute-start | bytes 393224 | tf_op jit(solution)/shard_map/while/body/eval_jaxpr/ppermute | solution.py:12
  180.6 4.4 %collective-permute-start = (bf16[256,2,128]{2,0,1:T(8,128)(2,1)S(1)}, bf16[256,2,128]{2,0,1:T(8,128)(2,1)S(1)}, u32[]{:S(2)}, u32[]{:S(2)}) collective-permute-start(bf16[256,2,128]{2,0,1:T(8,128)(2,1)S(1)} %get-tuple-element.505), channel_id=1, source_target_pairs={{0,8},{8,16},{16,24},{24,32},{32,40},{40,48},{48,56},{56,64},{64,7... | collective-permute-start | bytes 393224 | tf_op jit(solution)/shard_map/while/body/eval_jaxpr/ppermute | solution.py:12
  185.0 4.7 %collective-permute-start.3 = (f32[256,2,128]{2,0,1:T(8,128)}, f32[256,2,128]{2,0,1:T(8,128)S(1)}, u32[]{:S(2)}, u32[]{:S(2)}) collective-permute-start(f32[256,2,128]{2,0,1:T(8,128)} %get-tuple-element.508), channel_id=1, source_target_pairs={{0,8},{8,16},{16,24},{24,32},{32,40},{40,48},{48,56},{56,64},{64,7... | collective-permute-start | bytes 786440 | tf_op jit(solution)/shard_map/while/body/eval_jaxpr/ppermute | solution.py:17
  189.7 5.6 %collective-permute-start.2 = (f32[256,2,128]{2,0,1:T(8,128)S(1)}, f32[256,2,128]{2,0,1:T(8,128)S(1)}, u32[]{:S(2)}, u32[]{:S(2)}) collective-permute-start(f32[256,2,128]{2,0,1:T(8,128)S(1)} %get-tuple-element.507), channel_id=1, source_target_pairs={{0,8},{8,16},{16,24},{24,32},{32,40},{40,48},{48,56},{56,64},{64,7... | collective-permute-start | bytes 786440 | tf_op jit(solution)/shard_map/while/body/eval_jaxpr/ppermute | solution.py:17
  207.6 12.0 %collective-permute-done.5 = bf16[256,2,128]{2,0,1:T(8,128)(2,1)S(1)} collective-permute-done((bf16[256,2,128]{2,0,1:T(8,128)(2,1)S(1)}, bf16[256,2,128]{2,0,1:T(8,128)(2,1)S(1)}, u32[]{:S(2)}, u32[]{:S(2)}) %collective-permute-start.5) | collective-permute-done | bytes 131104 | tf_op jit(solution)/shard_map/ppermute | solution.py:17
  (170 shorter events, 86.3 us)
Async XLA Ops:
  16.7 15.5 %collective-permute-start.1 = (bf16[256,2,128]{2,0,1:T(8,128)(2,1)S(1)}, bf16[256,2,128]{2,0,1:T(8,128)(2,1)S(1)}, u32[]{:S(2)}, u32[]{:S(2)}) collective-permute-start(bf16[256,2,128]{2,0,1:T(8,128)(2,1)S(1)} %get-tuple-element.506), channel_id=1, source_target_pairs={{0,8},{8,16},{16,24},{24,32},{32,40},{40,48},{48,56},{56,64},{64,7... | collective-permute-start | bytes 393224 | tf_op jit(solution)/shard_map/while/body/eval_jaxpr/ppermute | solution.py:12
  20.2 12.0 %collective-permute-start = (bf16[256,2,128]{2,0,1:T(8,128)(2,1)S(1)}, bf16[256,2,128]{2,0,1:T(8,128)(2,1)S(1)}, u32[]{:S(2)}, u32[]{:S(2)}) collective-permute-start(bf16[256,2,128]{2,0,1:T(8,128)(2,1)S(1)} %get-tuple-element.505), channel_id=1, source_target_pairs={{0,8},{8,16},{16,24},{24,32},{32,40},{40,48},{48,56},{56,64},{64,7... | collective-permute-start | bytes 393224 | tf_op jit(solution)/shard_map/while/body/eval_jaxpr/ppermute | solution.py:12
  23.7 13.5 %collective-permute-start.3 = (f32[256,2,128]{2,0,1:T(8,128)}, f32[256,2,128]{2,0,1:T(8,128)S(1)}, u32[]{:S(2)}, u32[]{:S(2)}) collective-permute-start(f32[256,2,128]{2,0,1:T(8,128)} %get-tuple-element.508), channel_id=1, source_target_pairs={{0,8},{8,16},{16,24},{24,32},{32,40},{40,48},{48,56},{56,64},{64,7... | collective-permute-start | bytes 786440 | tf_op jit(solution)/shard_map/while/body/eval_jaxpr/ppermute | solution.py:17
  27.2 13.8 %collective-permute-start.2 = (f32[256,2,128]{2,0,1:T(8,128)S(1)}, f32[256,2,128]{2,0,1:T(8,128)S(1)}, u32[]{:S(2)}, u32[]{:S(2)}) collective-permute-start(f32[256,2,128]{2,0,1:T(8,128)S(1)} %get-tuple-element.507), channel_id=1, source_target_pairs={{0,8},{8,16},{16,24},{24,32},{32,40},{40,48},{48,56},{56,64},{64,7... | collective-permute-start | bytes 786440 | tf_op jit(solution)/shard_map/while/body/eval_jaxpr/ppermute | solution.py:17
  41.4 13.6 %collective-permute-start.1 = (bf16[256,2,128]{2,0,1:T(8,128)(2,1)S(1)}, bf16[256,2,128]{2,0,1:T(8,128)(2,1)S(1)}, u32[]{:S(2)}, u32[]{:S(2)}) collective-permute-start(bf16[256,2,128]{2,0,1:T(8,128)(2,1)S(1)} %get-tuple-element.506), channel_id=1, source_target_pairs={{0,8},{8,16},{16,24},{24,32},{32,40},{40,48},{48,56},{56,64},{64,7... | collective-permute-start | bytes 393224 | tf_op jit(solution)/shard_map/while/body/eval_jaxpr/ppermute | solution.py:12
  43.4 11.7 %collective-permute-start = (bf16[256,2,128]{2,0,1:T(8,128)(2,1)S(1)}, bf16[256,2,128]{2,0,1:T(8,128)(2,1)S(1)}, u32[]{:S(2)}, u32[]{:S(2)}) collective-permute-start(bf16[256,2,128]{2,0,1:T(8,128)(2,1)S(1)} %get-tuple-element.505), channel_id=1, source_target_pairs={{0,8},{8,16},{16,24},{24,32},{32,40},{40,48},{48,56},{56,64},{64,7... | collective-permute-start | bytes 393224 | tf_op jit(solution)/shard_map/while/body/eval_jaxpr/ppermute | solution.py:12
  47.5 13.4 %collective-permute-start.3 = (f32[256,2,128]{2,0,1:T(8,128)}, f32[256,2,128]{2,0,1:T(8,128)S(1)}, u32[]{:S(2)}, u32[]{:S(2)}) collective-permute-start(f32[256,2,128]{2,0,1:T(8,128)} %get-tuple-element.508), channel_id=1, source_target_pairs={{0,8},{8,16},{16,24},{24,32},{32,40},{40,48},{48,56},{56,64},{64,7... | collective-permute-start | bytes 786440 | tf_op jit(solution)/shard_map/while/body/eval_jaxpr/ppermute | solution.py:17
  50.4 13.3 %collective-permute-start.2 = (f32[256,2,128]{2,0,1:T(8,128)S(1)}, f32[256,2,128]{2,0,1:T(8,128)S(1)}, u32[]{:S(2)}, u32[]{:S(2)}) collective-permute-start(f32[256,2,128]{2,0,1:T(8,128)S(1)} %get-tuple-element.507), channel_id=1, source_target_pairs={{0,8},{8,16},{16,24},{24,32},{32,40},{40,48},{48,56},{56,64},{64,7... | collective-permute-start | bytes 786440 | tf_op jit(solution)/shard_map/while/body/eval_jaxpr/ppermute | solution.py:17
  64.2 13.4 %collective-permute-start.1 = (bf16[256,2,128]{2,0,1:T(8,128)(2,1)S(1)}, bf16[256,2,128]{2,0,1:T(8,128)(2,1)S(1)}, u32[]{:S(2)}, u32[]{:S(2)}) collective-permute-start(bf16[256,2,128]{2,0,1:T(8,128)(2,1)S(1)} %get-tuple-element.506), channel_id=1, source_target_pairs={{0,8},{8,16},{16,24},{24,32},{32,40},{40,48},{48,56},{56,64},{64,7... | collective-permute-start | bytes 393224 | tf_op jit(solution)/shard_map/while/body/eval_jaxpr/ppermute | solution.py:12
  66.1 11.5 %collective-permute-start = (bf16[256,2,128]{2,0,1:T(8,128)(2,1)S(1)}, bf16[256,2,128]{2,0,1:T(8,128)(2,1)S(1)}, u32[]{:S(2)}, u32[]{:S(2)}) collective-permute-start(bf16[256,2,128]{2,0,1:T(8,128)(2,1)S(1)} %get-tuple-element.505), channel_id=1, source_target_pairs={{0,8},{8,16},{16,24},{24,32},{32,40},{40,48},{48,56},{56,64},{64,7... | collective-permute-start | bytes 393224 | tf_op jit(solution)/shard_map/while/body/eval_jaxpr/ppermute | solution.py:12
  69.6 13.5 %collective-permute-start.3 = (f32[256,2,128]{2,0,1:T(8,128)}, f32[256,2,128]{2,0,1:T(8,128)S(1)}, u32[]{:S(2)}, u32[]{:S(2)}) collective-permute-start(f32[256,2,128]{2,0,1:T(8,128)} %get-tuple-element.508), channel_id=1, source_target_pairs={{0,8},{8,16},{16,24},{24,32},{32,40},{40,48},{48,56},{56,64},{64,7... | collective-permute-start | bytes 786440 | tf_op jit(solution)/shard_map/while/body/eval_jaxpr/ppermute | solution.py:17
  73.2 13.1 %collective-permute-start.2 = (f32[256,2,128]{2,0,1:T(8,128)S(1)}, f32[256,2,128]{2,0,1:T(8,128)S(1)}, u32[]{:S(2)}, u32[]{:S(2)}) collective-permute-start(f32[256,2,128]{2,0,1:T(8,128)S(1)} %get-tuple-element.507), channel_id=1, source_target_pairs={{0,8},{8,16},{16,24},{24,32},{32,40},{40,48},{48,56},{56,64},{64,7... | collective-permute-start | bytes 786440 | tf_op jit(solution)/shard_map/while/body/eval_jaxpr/ppermute | solution.py:17
  86.8 13.4 %collective-permute-start.1 = (bf16[256,2,128]{2,0,1:T(8,128)(2,1)S(1)}, bf16[256,2,128]{2,0,1:T(8,128)(2,1)S(1)}, u32[]{:S(2)}, u32[]{:S(2)}) collective-permute-start(bf16[256,2,128]{2,0,1:T(8,128)(2,1)S(1)} %get-tuple-element.506), channel_id=1, source_target_pairs={{0,8},{8,16},{16,24},{24,32},{32,40},{40,48},{48,56},{56,64},{64,7... | collective-permute-start | bytes 393224 | tf_op jit(solution)/shard_map/while/body/eval_jaxpr/ppermute | solution.py:12
  88.7 11.5 %collective-permute-start = (bf16[256,2,128]{2,0,1:T(8,128)(2,1)S(1)}, bf16[256,2,128]{2,0,1:T(8,128)(2,1)S(1)}, u32[]{:S(2)}, u32[]{:S(2)}) collective-permute-start(bf16[256,2,128]{2,0,1:T(8,128)(2,1)S(1)} %get-tuple-element.505), channel_id=1, source_target_pairs={{0,8},{8,16},{16,24},{24,32},{32,40},{40,48},{48,56},{56,64},{64,7... | collective-permute-start | bytes 393224 | tf_op jit(solution)/shard_map/while/body/eval_jaxpr/ppermute | solution.py:12
  91.8 13.5 %collective-permute-start.3 = (f32[256,2,128]{2,0,1:T(8,128)}, f32[256,2,128]{2,0,1:T(8,128)S(1)}, u32[]{:S(2)}, u32[]{:S(2)}) collective-permute-start(f32[256,2,128]{2,0,1:T(8,128)} %get-tuple-element.508), channel_id=1, source_target_pairs={{0,8},{8,16},{16,24},{24,32},{32,40},{40,48},{48,56},{56,64},{64,7... | collective-permute-start | bytes 786440 | tf_op jit(solution)/shard_map/while/body/eval_jaxpr/ppermute | solution.py:17
  95.5 13.0 %collective-permute-start.2 = (f32[256,2,128]{2,0,1:T(8,128)S(1)}, f32[256,2,128]{2,0,1:T(8,128)S(1)}, u32[]{:S(2)}, u32[]{:S(2)}) collective-permute-start(f32[256,2,128]{2,0,1:T(8,128)S(1)} %get-tuple-element.507), channel_id=1, source_target_pairs={{0,8},{8,16},{16,24},{24,32},{32,40},{40,48},{48,56},{56,64},{64,7... | collective-permute-start | bytes 786440 | tf_op jit(solution)/shard_map/while/body/eval_jaxpr/ppermute | solution.py:17
  108.9 15.6 %collective-permute-start.1 = (bf16[256,2,128]{2,0,1:T(8,128)(2,1)S(1)}, bf16[256,2,128]{2,0,1:T(8,128)(2,1)S(1)}, u32[]{:S(2)}, u32[]{:S(2)}) collective-permute-start(bf16[256,2,128]{2,0,1:T(8,128)(2,1)S(1)} %get-tuple-element.506), channel_id=1, source_target_pairs={{0,8},{8,16},{16,24},{24,32},{32,40},{40,48},{48,56},{56,64},{64,7... | collective-permute-start | bytes 393224 | tf_op jit(solution)/shard_map/while/body/eval_jaxpr/ppermute | solution.py:12
  110.9 13.7 %collective-permute-start = (bf16[256,2,128]{2,0,1:T(8,128)(2,1)S(1)}, bf16[256,2,128]{2,0,1:T(8,128)(2,1)S(1)}, u32[]{:S(2)}, u32[]{:S(2)}) collective-permute-start(bf16[256,2,128]{2,0,1:T(8,128)(2,1)S(1)} %get-tuple-element.505), channel_id=1, source_target_pairs={{0,8},{8,16},{16,24},{24,32},{32,40},{40,48},{48,56},{56,64},{64,7... | collective-permute-start | bytes 393224 | tf_op jit(solution)/shard_map/while/body/eval_jaxpr/ppermute | solution.py:12
  114.2 13.5 %collective-permute-start.3 = (f32[256,2,128]{2,0,1:T(8,128)}, f32[256,2,128]{2,0,1:T(8,128)S(1)}, u32[]{:S(2)}, u32[]{:S(2)}) collective-permute-start(f32[256,2,128]{2,0,1:T(8,128)} %get-tuple-element.508), channel_id=1, source_target_pairs={{0,8},{8,16},{16,24},{24,32},{32,40},{40,48},{48,56},{56,64},{64,7... | collective-permute-start | bytes 786440 | tf_op jit(solution)/shard_map/while/body/eval_jaxpr/ppermute | solution.py:17
  118.6 12.0 %collective-permute-start.2 = (f32[256,2,128]{2,0,1:T(8,128)S(1)}, f32[256,2,128]{2,0,1:T(8,128)S(1)}, u32[]{:S(2)}, u32[]{:S(2)}) collective-permute-start(f32[256,2,128]{2,0,1:T(8,128)S(1)} %get-tuple-element.507), channel_id=1, source_target_pairs={{0,8},{8,16},{16,24},{24,32},{32,40},{40,48},{48,56},{56,64},{64,7... | collective-permute-start | bytes 786440 | tf_op jit(solution)/shard_map/while/body/eval_jaxpr/ppermute | solution.py:17
  131.0 17.2 %collective-permute-start.1 = (bf16[256,2,128]{2,0,1:T(8,128)(2,1)S(1)}, bf16[256,2,128]{2,0,1:T(8,128)(2,1)S(1)}, u32[]{:S(2)}, u32[]{:S(2)}) collective-permute-start(bf16[256,2,128]{2,0,1:T(8,128)(2,1)S(1)} %get-tuple-element.506), channel_id=1, source_target_pairs={{0,8},{8,16},{16,24},{24,32},{32,40},{40,48},{48,56},{56,64},{64,7... | collective-permute-start | bytes 393224 | tf_op jit(solution)/shard_map/while/body/eval_jaxpr/ppermute | solution.py:12
  133.1 15.1 %collective-permute-start = (bf16[256,2,128]{2,0,1:T(8,128)(2,1)S(1)}, bf16[256,2,128]{2,0,1:T(8,128)(2,1)S(1)}, u32[]{:S(2)}, u32[]{:S(2)}) collective-permute-start(bf16[256,2,128]{2,0,1:T(8,128)(2,1)S(1)} %get-tuple-element.505), channel_id=1, source_target_pairs={{0,8},{8,16},{16,24},{24,32},{32,40},{40,48},{48,56},{56,64},{64,7... | collective-permute-start | bytes 393224 | tf_op jit(solution)/shard_map/while/body/eval_jaxpr/ppermute | solution.py:12
  137.8 12.9 %collective-permute-start.3 = (f32[256,2,128]{2,0,1:T(8,128)}, f32[256,2,128]{2,0,1:T(8,128)S(1)}, u32[]{:S(2)}, u32[]{:S(2)}) collective-permute-start(f32[256,2,128]{2,0,1:T(8,128)} %get-tuple-element.508), channel_id=1, source_target_pairs={{0,8},{8,16},{16,24},{24,32},{32,40},{40,48},{48,56},{56,64},{64,7... | collective-permute-start | bytes 786440 | tf_op jit(solution)/shard_map/while/body/eval_jaxpr/ppermute | solution.py:17
  142.3 11.0 %collective-permute-start.2 = (f32[256,2,128]{2,0,1:T(8,128)S(1)}, f32[256,2,128]{2,0,1:T(8,128)S(1)}, u32[]{:S(2)}, u32[]{:S(2)}) collective-permute-start(f32[256,2,128]{2,0,1:T(8,128)S(1)} %get-tuple-element.507), channel_id=1, source_target_pairs={{0,8},{8,16},{16,24},{24,32},{32,40},{40,48},{48,56},{56,64},{64,7... | collective-permute-start | bytes 786440 | tf_op jit(solution)/shard_map/while/body/eval_jaxpr/ppermute | solution.py:17
  153.8 18.2 %collective-permute-start.1 = (bf16[256,2,128]{2,0,1:T(8,128)(2,1)S(1)}, bf16[256,2,128]{2,0,1:T(8,128)(2,1)S(1)}, u32[]{:S(2)}, u32[]{:S(2)}) collective-permute-start(bf16[256,2,128]{2,0,1:T(8,128)(2,1)S(1)} %get-tuple-element.506), channel_id=1, source_target_pairs={{0,8},{8,16},{16,24},{24,32},{32,40},{40,48},{48,56},{56,64},{64,7... | collective-permute-start | bytes 393224 | tf_op jit(solution)/shard_map/while/body/eval_jaxpr/ppermute | solution.py:12
  156.9 15.1 %collective-permute-start = (bf16[256,2,128]{2,0,1:T(8,128)(2,1)S(1)}, bf16[256,2,128]{2,0,1:T(8,128)(2,1)S(1)}, u32[]{:S(2)}, u32[]{:S(2)}) collective-permute-start(bf16[256,2,128]{2,0,1:T(8,128)(2,1)S(1)} %get-tuple-element.505), channel_id=1, source_target_pairs={{0,8},{8,16},{16,24},{24,32},{32,40},{40,48},{48,56},{56,64},{64,7... | collective-permute-start | bytes 393224 | tf_op jit(solution)/shard_map/while/body/eval_jaxpr/ppermute | solution.py:12
  161.3 13.1 %collective-permute-start.3 = (f32[256,2,128]{2,0,1:T(8,128)}, f32[256,2,128]{2,0,1:T(8,128)S(1)}, u32[]{:S(2)}, u32[]{:S(2)}) collective-permute-start(f32[256,2,128]{2,0,1:T(8,128)} %get-tuple-element.508), channel_id=1, source_target_pairs={{0,8},{8,16},{16,24},{24,32},{32,40},{40,48},{48,56},{56,64},{64,7... | collective-permute-start | bytes 786440 | tf_op jit(solution)/shard_map/while/body/eval_jaxpr/ppermute | solution.py:17
  177.5 18.1 %collective-permute-start.1 = (bf16[256,2,128]{2,0,1:T(8,128)(2,1)S(1)}, bf16[256,2,128]{2,0,1:T(8,128)(2,1)S(1)}, u32[]{:S(2)}, u32[]{:S(2)}) collective-permute-start(bf16[256,2,128]{2,0,1:T(8,128)(2,1)S(1)} %get-tuple-element.506), channel_id=1, source_target_pairs={{0,8},{8,16},{16,24},{24,32},{32,40},{40,48},{48,56},{56,64},{64,7... | collective-permute-start | bytes 393224 | tf_op jit(solution)/shard_map/while/body/eval_jaxpr/ppermute | solution.py:12
  180.6 15.1 %collective-permute-start = (bf16[256,2,128]{2,0,1:T(8,128)(2,1)S(1)}, bf16[256,2,128]{2,0,1:T(8,128)(2,1)S(1)}, u32[]{:S(2)}, u32[]{:S(2)}) collective-permute-start(bf16[256,2,128]{2,0,1:T(8,128)(2,1)S(1)} %get-tuple-element.505), channel_id=1, source_target_pairs={{0,8},{8,16},{16,24},{24,32},{32,40},{40,48},{48,56},{56,64},{64,7... | collective-permute-start | bytes 393224 | tf_op jit(solution)/shard_map/while/body/eval_jaxpr/ppermute | solution.py:12
  185.0 13.1 %collective-permute-start.3 = (f32[256,2,128]{2,0,1:T(8,128)}, f32[256,2,128]{2,0,1:T(8,128)S(1)}, u32[]{:S(2)}, u32[]{:S(2)}) collective-permute-start(f32[256,2,128]{2,0,1:T(8,128)} %get-tuple-element.508), channel_id=1, source_target_pairs={{0,8},{8,16},{16,24},{24,32},{32,40},{40,48},{48,56},{56,64},{64,7... | collective-permute-start | bytes 786440 | tf_op jit(solution)/shard_map/while/body/eval_jaxpr/ppermute | solution.py:17
  202.1 17.6 %collective-permute-start.5 = (bf16[256,2,128]{2,0,1:T(8,128)(2,1)S(1)}, bf16[256,2,128]{2,0,1:T(8,128)(2,1)S(1)}, u32[]{:S(2)}, u32[]{:S(2)}) collective-permute-start(bf16[256,2,128]{2,0,1:T(8,128)(2,1)S(1)} %convert_element_type.66), channel_id=1, source_target_pairs={{0,448},{8,456},{16,464},{24,472},{32,480},{40,488},{48,496},{56,5... | collective-permute-start | bytes 393224 | tf_op jit(solution)/shard_map/ppermute | solution.py:17
  204.0 17.0 %collective-permute-start.4 = (bf16[256,2,128]{2,0,1:T(8,128)(2,1)S(1)}, bf16[256,2,128]{2,0,1:T(8,128)(2,1)S(1)}, u32[]{:S(2)}, u32[]{:S(2)}) collective-permute-start(bf16[256,2,128]{2,0,1:T(8,128)(2,1)S(1)} %convert_element_type.62), channel_id=1, source_target_pairs={{0,448},{8,456},{16,464},{24,472},{32,480},{40,488},{48,496},{56,5... | collective-permute-start | bytes 393224 | tf_op jit(solution)/shard_map/ppermute | solution.py:17
  (4 other events, 30.7 us)
where the time goes:
time: 223 us; the launch traced here: 222 us
  starting transfers between devices  126 us (57%)
  waiting for transfers between devices  39.6 us (18%)
  matrix products  35.1 us (16%)
  local copies, waits for them, and re-layouts  12.1 us (5%)
  other arithmetic  6.94 us (3%)
    ppermute x18, starting transfers between devices, shifted(): lax.ppermute(array, axis, [(i, (i + by) % length) for i in range(length)])  75.4 us
    ppermute x16, starting transfers between devices, passed_along(): lax.ppermute(value, axis, [(source, source + steps) for source in range(f...  50.5 us
    ppermute x18, waiting for transfers between devices, shifted(): lax.ppermute(array, axis, [(i, (i + by) % length) for i in range(length)])  39.6 us
    dot_general x9, matrix products, tile_terms(): jnp.einsum('wmax,pmx->mawp', query_rows, key_block_slice, preferred_eleme...  10.9 us
    dot_general x9, matrix products, tile_terms(): jnp.einsum('vfiy,ivfq->yvq', probability_block, output_gradient_rows, pre...  10.3 us
    dot_general x9, matrix products, tile_terms(): jnp.einsum('vyxz,zvh->xvyh', score_gradient, key_block_slice, preferred_e...  6.1 us
    unnamed x13, local copies, waits for them, and re-layouts  4.72 us
  transfers between devices with their start and end apart: 34, of which 15 were waited for; matrix products, arithmetic and copies ran while one was open for 15% of the time, Pallas kernels for 0%

commit v1 on v0

v1 whole, which is shorter than its diff:
```python
import functools
import math

import jax
import jax.numpy as jnp
from jax import lax
from jax.experimental import pallas as pl
from jax.experimental.pallas import tpu as pltpu
from jax.sharding import PartitionSpec as P

HEAD_WIDTH = 128
LOG2_E = math.log2(math.e)


def moved(array, by):
    count = lax.axis_size("ctx")
    return lax.ppermute(array, "ctx", [(i, (i + by) % count) for i in range(count)])


def doc_starts(index_ref, lengths_ref, rows):
    first = index_ref[0] * rows
    places = first + lax.broadcasted_iota(jnp.int32, (1, rows), 1)
    start = jnp.zeros((1, rows), jnp.int32)
    end = jnp.int32(0)
    for doc in range(lengths_ref.shape[0]):
        end = end + lengths_ref[doc]
        start = jnp.where(places >= end, end, start)
    return start - first


def transposed_dot(a, b):
    return lax.dot_general(a, b, (((1,), (1,)), ((), ())), preferred_element_type=jnp.float32)


def one_block(distance, starts, q, do, lse, delta, kv, dq, dkv):
    rows, width = q.shape[0], HEAD_WIDTH
    groups = kv.shape[1] // (2 * width)
    per_group = q.shape[1] // (groups * width)
    key = lax.broadcasted_iota(jnp.int32, (rows, rows), 0)
    live = key - distance * rows >= starts
    if distance == 0:
        live &= key <= lax.broadcasted_iota(jnp.int32, (rows, rows), 1)
    scale = LOG2_E * width**-0.5
    for group in range(groups):
        k = kv[:, pl.ds(group * width, width)]
        v = kv[:, pl.ds((groups + group) * width, width)]
        k_t = k.T
        dk = dv = None
        for head in range(group * per_group, (group + 1) * per_group):
            columns = pl.ds(head * width, width)
            q_h, do_h = q[:, columns], do[:, columns]
            score = transposed_dot(k, q_h) * scale - lse[pl.ds(head, 1), :] * LOG2_E
            prob = jnp.where(live, jnp.exp2(score), 0.0)
            dscore = prob * (transposed_dot(v, do_h) - delta[pl.ds(head, 1), :])
            prob, dscore = prob.astype(jnp.bfloat16), dscore.astype(jnp.bfloat16)
            dv_h = jnp.dot(prob, do_h, preferred_element_type=jnp.float32)
            dk_h = jnp.dot(dscore, q_h, preferred_element_type=jnp.float32)
            dk, dv = (dk_h, dv_h) if dk is None else (dk + dk_h, dv + dv_h)
            dq_h = jnp.dot(k_t, dscore, preferred_element_type=jnp.float32)
            if distance == 0:
                dq[columns, :] = dq_h
            else:
                dq[columns, :] += dq_h
        dkv[:, pl.ds(group * width, width)] = dk.astype(dkv.dtype)
        dkv[:, pl.ds((groups + group) * width, width)] = dv.astype(dkv.dtype)


def own_kernel(index, lengths, q, do, o, lse, kv, dq, dkv, delta):
    rows, heads = q.shape[0], lse.shape[0]
    lane = lax.broadcasted_iota(jnp.int32, (rows, HEAD_WIDTH), 1)
    sums = jnp.zeros((rows, HEAD_WIDTH), jnp.float32)
    for head in range(heads):
        columns = pl.ds(head * HEAD_WIDTH, HEAD_WIDTH)
        product = do[:, columns].astype(jnp.float32) * o[:, columns].astype(jnp.float32)
        sums = jnp.where(lane == head, jnp.sum(product, axis=1, keepdims=True), sums)
    delta[...] = sums.T[:heads]
    one_block(0, doc_starts(index, lengths, rows), q, do, lse, delta, kv, dq, dkv)


def pair_kernel(distances, index, lengths, q, do, lse, delta, kv_a, kv_b, dq_in, dq, dkv_a, dkv_b):
    starts = doc_starts(index, lengths, q.shape[0])
    dq[...] = dq_in[...]
    for distance, kv, dkv in zip(distances, (kv_a, kv_b), (dkv_a, dkv_b)):
        one_block(distance, starts, q, do, lse, delta, kv, dq, dkv)


def turn_kernel(dq_t, dq):
    for head in range(dq.shape[1] // HEAD_WIDTH):
        columns = pl.ds(head * HEAD_WIDTH, HEAD_WIDTH)
        dq[:, columns] = (dq_t[columns, :].T * HEAD_WIDTH**-0.5).astype(dq.dtype)


VMEM = pl.BlockSpec(memory_space=pltpu.VMEM)
SMEM = pl.BlockSpec(memory_space=pltpu.SMEM)


def call(kernel, name, scalars, arrays, outs, blocks, rows, heads):
    return pl.pallas_call(
        kernel,
        name=name,
        out_shape=outs,
        in_specs=[SMEM] * scalars + [VMEM] * (arrays - scalars),
        out_specs=[VMEM] * len(outs),
        cost_estimate=pl.CostEstimate(
            flops=2 * 10 * blocks * heads * rows * rows * HEAD_WIDTH,
            bytes_accessed=4 << 20,
            transcendentals=blocks * heads * rows * rows,
        ),
        compiler_params=pltpu.CompilerParams(vmem_limit_bytes=32 << 20),
    )


def body(query, keys, values, output, output_gradient, row_log_norm, doc_lengths):
    rows, heads = query.shape[0], row_log_norm.shape[0]
    scale = HEAD_WIDTH**-0.5
    index = lax.axis_index("ctx").astype(jnp.int32).reshape(1)
    kv = jnp.concatenate([keys, values], axis=1)
    dq_shape = jax.ShapeDtypeStruct((query.shape[1], rows), jnp.float32)
    part_shape = jax.ShapeDtypeStruct(kv.shape, jnp.bfloat16)

    up, down = [kv], [moved(kv, 8)]
    for _ in range(4):
        up.append(moved(up[-1], 1))
    for _ in range(3):
        down.append(moved(down[-1], -1))

    dq, own, delta = call(
        own_kernel,
        "own_block",
        2,
        7,
        [
            dq_shape,
            jax.ShapeDtypeStruct(kv.shape, jnp.float32),
            jax.ShapeDtypeStruct((heads, rows), jnp.float32),
        ],
        1,
        rows,
        heads,
    )(index, doc_lengths, query, output_gradient, output, row_log_norm, kv)
    parts = {}
    for near in range(1, 5):
        far = 9 - near
        dq, parts[near], parts[far] = call(
            functools.partial(pair_kernel, (near, far)),
            f"blocks_{near}_{far}",
            2,
            9,
            [dq_shape, part_shape, part_shape],
            2,
            rows,
            heads,
        )(
            index,
            doc_lengths,
            query,
            output_gradient,
            row_log_norm,
            delta,
            up[near],
            down[near - 1],
            dq,
        )

    def joined(a, b):
        return (a.astype(jnp.float32) + b.astype(jnp.float32)).astype(jnp.bfloat16)

    near, far = parts[4], parts[5]
    for step in range(1, 4):
        near = joined(moved(near, -1), parts[4 - step])
        far = joined(moved(far, 1), parts[5 + step])
    near, far = moved(near, -1), moved(far, -8)
    total = own + near.astype(jnp.float32) + far.astype(jnp.float32)

    (grad_query,) = call(
        turn_kernel,
        "turn_query_gradient",
        0,
        1,
        [jax.ShapeDtypeStruct(query.shape, jnp.bfloat16)],
        0,
        rows,
        heads,
    )(dq)
    split = keys.shape[1]
    key_gradient = (scale * total[:, :split]).astype(jnp.bfloat16)
    value_gradient = total[:, split:].astype(jnp.bfloat16)
    return grad_query, key_gradient, value_gradient


def solution(mesh):
    tokens = P(("dp", "ctx"), "head")
    return jax.shard_map(
        body,
        mesh=mesh,
        in_specs=(tokens,) * 5 + (P("head", ("dp", "ctx")), P("dp")),
        out_specs=(tokens,) * 3,
        check_vma=False,
    )
```

time: 223 us -> 127 us (0.57)
  the two profiles are of different devices: /device:TPU:198 before, /device:TPU:6 now
where the time goes in v1:
time: 127 us; the launch traced here: 126 us
  starting transfers between devices  67.3 us (53%)
  waiting for transfers between devices  29.2 us (23%)
  Pallas kernels  23 us (18%)
  local copies, waits for them, and re-layouts  4.66 us (4%)
    ppermute x16, starting transfers between devices, moved(): lax.ppermute(array, 'ctx', [(i, (i + by) % count) for i in range(count)])  67.3 us
    ppermute x16, waiting for transfers between devices, moved(): lax.ppermute(array, 'ctx', [(i, (i + by) % count) for i in range(count)])  29.2 us
    pallas_call x4, Pallas kernels, body(): call(functools.partial(pair_kernel, (near, far)), f'blocks_{near}_{far}',...  19 us
    unnamed x13, local copies, waits for them, and re-layouts  3.07 us
    pallas_call x1, Pallas kernels, body(): call(own_kernel, 'own_block', 2, 7, [dq_shape, jax.ShapeDtypeStruct(kv.sh...  2.92 us
  transfers between devices with their start and end apart: 16, of which 7 were waited for; matrix products, arithmetic and copies ran while one was open for 0% of the time, Pallas kernels for 14%

profile of v1, /device:TPU:6, one launch (start us, length us, event | category | flops | bytes accessed | tf_op | source)
XLA Modules:
  0.0 126.3 jit_solution(12626065103606738098)
XLA Ops:
  0.6 1.0 constant_dynamic-update-slice_fusion.1
  1.6 0.9 constant_dynamic-update-slice_fusion.kv
  2.5 4.3 %collective-permute-start.4 = (bf16[256,512]{1,0:T(8,128)(2,1)S(1)}, bf16[256,512]{1,0:T(8,128)(2,1)S(1)}, u32[]{:S(2)}, u32[]{:S(2)}) collective-permute-start(bf16[256,512]{1,0:T(8,128)(2,1)S(1)} %constant_dynamic-update-slice_fusion.kv), channel_id=1, source_target_pairs={{0,64},{8,72},{16,80},{24,88},{32,96},{40,104},{48,112},{56,120},{... | collective-permute-start | bytes 786440 | tf_op jit(solution)/shard_map/ppermute | solution.py:17
  6.8 3.5 %collective-permute-start = (bf16[256,512]{1,0:T(8,128)(2,1)S(1)}, bf16[256,512]{1,0:T(8,128)(2,1)S(1)}, u32[]{:S(2)}, u32[]{:S(2)}) collective-permute-start(bf16[256,512]{1,0:T(8,128)(2,1)S(1)} %constant_dynamic-update-slice_fusion.kv), channel_id=1, source_target_pairs={{0,8},{8,16},{16,24},{24,32},{32,40},{40,48},{48,56},{56,64},{64,7... | collective-permute-start | bytes 786440 | tf_op jit(solution)/shard_map/ppermute | solution.py:17
  10.3 15.1 %collective-permute-done.4.kv_b = bf16[256,512]{1,0:T(8,128)(2,1)S(1)} collective-permute-done((bf16[256,512]{1,0:T(8,128)(2,1)S(1)}, bf16[256,512]{1,0:T(8,128)(2,1)S(1)}, u32[]{:S(2)}, u32[]{:S(2)}) %collective-permute-start.4) | collective-permute-done | bytes 262176 | tf_op jit(solution)/shard_map/ppermute | solution.py:17
  25.4 1.9 %collective-permute-start.5 = (bf16[256,512]{1,0:T(8,128)(2,1)S(1)}, bf16[256,512]{1,0:T(8,128)(2,1)S(1)}, u32[]{:S(2)}, u32[]{:S(2)}) collective-permute-start(bf16[256,512]{1,0:T(8,128)(2,1)S(1)} %collective-permute-done.4.kv_b), channel_id=1, source_target_pairs={{0,504},{8,0},{16,8},{24,16},{32,24},{40,32},{48,40},{56,48},{64,5... | collective-permute-start | bytes 786440 | tf_op jit(solution)/shard_map/ppermute | solution.py:17
  27.3 3.9 %collective-permute-start.1 = (bf16[256,512]{1,0:T(8,128)(2,1)S(1)}, bf16[256,512]{1,0:T(8,128)(2,1)S(1)}, u32[]{:S(2)}, u32[]{:S(2)}) collective-permute-start(bf16[256,512]{1,0:T(8,128)(2,1)S(1)} %collective-permute-done.kv_a), channel_id=1, source_target_pairs={{0,8},{8,16},{16,24},{24,32},{32,40},{40,48},{48,56},{56,64},{64,7... | collective-permute-start | bytes 786440 | tf_op jit(solution)/shard_map/ppermute | solution.py:17
  31.3 3.2 %collective-permute-done.5.kv_b = bf16[256,512]{1,0:T(8,128)(2,1)S(1)} collective-permute-done((bf16[256,512]{1,0:T(8,128)(2,1)S(1)}, bf16[256,512]{1,0:T(8,128)(2,1)S(1)}, u32[]{:S(2)}, u32[]{:S(2)}) %collective-permute-start.5) | collective-permute-done | bytes 262176 | tf_op jit(solution)/shard_map/ppermute | solution.py:17
  34.5 4.4 %collective-permute-start.6 = (bf16[256,512]{1,0:T(8,128)(2,1)S(1)}, bf16[256,512]{1,0:T(8,128)(2,1)S(1)}, u32[]{:S(2)}, u32[]{:S(2)}) collective-permute-start(bf16[256,512]{1,0:T(8,128)(2,1)S(1)} %collective-permute-done.5.kv_b), channel_id=1, source_target_pairs={{0,504},{8,0},{16,8},{24,16},{32,24},{40,32},{48,40},{56,48},{64,5... | collective-permute-start | bytes 786440 | tf_op jit(solution)/shard_map/ppermute | solution.py:17
  38.9 1.9 %collective-permute-start.2 = (bf16[256,512]{1,0:T(8,128)(2,1)S(1)}, bf16[256,512]{1,0:T(8,128)(2,1)S(1)}, u32[]{:S(2)}, u32[]{:S(2)}) collective-permute-start(bf16[256,512]{1,0:T(8,128)(2,1)S(1)} %collective-permute-done.1.kv_a), channel_id=1, source_target_pairs={{0,8},{8,16},{16,24},{24,32},{32,40},{40,48},{48,56},{56,64},{64,7... | collective-permute-start | bytes 786440 | tf_op jit(solution)/shard_map/ppermute | solution.py:17
  40.9 1.0 copy-done.1
  41.9 1.0 copy-done.2
  43.0 2.9 %own_block.1 = (f32[1024,256]{1,0:T(8,128)S(1)}, f32[256,512]{1,0:T(8,128)S(1)}, f32[8,256]{1,0:T(8,128)S(1)}) custom-call(s32[1]{0:T(128)} %bitcast.index, s32[16]{0:T(128)S(1)} %copy-done.5, bf16[256,1024]{1,0:T(8,128)(2,1)S(1)} %copy-done.1, bf16[256,1024]{1,0:T(8,128)(2,1)S(1)} %copy-done.2, bf16[256,1024]{1,0:T(8,128)(2,1)S(1)} %copy-done, ...), custom_call_target="tpu_custom_call" | custom-call | flops 1342177280 | bytes 4194304 | tf_op jit(solution)/shard_map/own_block/pallas_call | solution.py:127
  45.9 4.7 %blocks_1_8.1 = (f32[1024,256]{1,0:T(8,128)S(1)}, bf16[256,512]{1,0:T(8,128)(2,1)S(1)}, bf16[256,512]{1,0:T(8,128)(2,1)S(1)}) custom-call(s32[1]{0:T(128)} %bitcast.index, s32[16]{0:T(128)S(1)} %copy-done.5, bf16[256,1024]{1,0:T(8,128)(2,1)S(1)} %copy-done.1, bf16[256,1024]{1,0:T(8,128)(2,1)S(1)} %copy-done.3, f32[8,256]{1,0:T(8,128)S(1)} %copy-done.4, ...), custom_call_target="tpu_custom_call" | custom-call | flops 2684354560 | bytes 4194304 | tf_op jit(solution)/shard_map/blocks_1_8/pallas_call | solution.py:144
  50.7 7.2 %collective-permute-start.7 = (bf16[256,512]{1,0:T(8,128)(2,1)S(1)}, bf16[256,512]{1,0:T(8,128)(2,1)S(1)}, u32[]{:S(2)}, u32[]{:S(2)}) collective-permute-start(bf16[256,512]{1,0:T(8,128)(2,1)S(1)} %collective-permute-done.6.kv_b), channel_id=1, source_target_pairs={{0,504},{8,0},{16,8},{24,16},{32,24},{40,32},{48,40},{56,48},{64,5... | collective-permute-start | bytes 786440 | tf_op jit(solution)/shard_map/ppermute | solution.py:17
  57.9 2.1 %collective-permute-start.3 = (bf16[256,512]{1,0:T(8,128)(2,1)S(1)}, bf16[256,512]{1,0:T(8,128)(2,1)S(1)}, u32[]{:S(2)}, u32[]{:S(2)}) collective-permute-start(bf16[256,512]{1,0:T(8,128)(2,1)S(1)} %collective-permute-done.2.kv_a), channel_id=1, source_target_pairs={{0,8},{8,16},{16,24},{24,32},{32,40},{40,48},{48,56},{56,64},{64,7... | collective-permute-start | bytes 786440 | tf_op jit(solution)/shard_map/ppermute | solution.py:17
  60.0 4.7 %blocks_2_7.1 = (f32[1024,256]{1,0:T(8,128)S(1)}, bf16[256,512]{1,0:T(8,128)(2,1)S(1)}, bf16[256,512]{1,0:T(8,128)(2,1)S(1)}) custom-call(s32[1]{0:T(128)} %bitcast.index, s32[16]{0:T(128)S(1)} %copy-done.5, bf16[256,1024]{1,0:T(8,128)(2,1)S(1)} %copy-done.1, bf16[256,1024]{1,0:T(8,128)(2,1)S(1)} %copy-done.3, f32[8,256]{1,0:T(8,128)S(1)} %copy-done.4, ...), custom_call_target="tpu_custom_call" | custom-call | flops 2684354560 | bytes 4194304 | tf_op jit(solution)/shard_map/blocks_2_7/pallas_call | solution.py:144
  64.8 4.7 %blocks_3_6.1 = (f32[1024,256]{1,0:T(8,128)S(1)}, bf16[256,512]{1,0:T(8,128)(2,1)S(1)}, bf16[256,512]{1,0:T(8,128)(2,1)S(1)}) custom-call(s32[1]{0:T(128)} %bitcast.index, s32[16]{0:T(128)S(1)} %copy-done.5, bf16[256,1024]{1,0:T(8,128)(2,1)S(1)} %copy-done.1, bf16[256,1024]{1,0:T(8,128)(2,1)S(1)} %copy-done.3, f32[8,256]{1,0:T(8,128)S(1)} %copy-done.4, ...), custom_call_target="tpu_custom_call" | custom-call | flops 2684354560 | bytes 4194304 | tf_op jit(solution)/shard_map/blocks_3_6/pallas_call | solution.py:144
  69.6 4.7 %blocks_4_5.1 = (f32[1024,256]{1,0:T(8,128)S(1)}, bf16[256,512]{1,0:T(8,128)(2,1)S(1)}, bf16[256,512]{1,0:T(8,128)(2,1)S(1)}) custom-call(s32[1]{0:T(128)} %bitcast.index, s32[16]{0:T(128)S(1)} %copy-done.5, bf16[256,1024]{1,0:T(8,128)(2,1)S(1)} %copy-done.1, bf16[256,1024]{1,0:T(8,128)(2,1)S(1)} %copy-done.3, f32[8,256]{1,0:T(8,128)S(1)} %copy-done.4, ...), custom_call_target="tpu_custom_call" | custom-call | flops 2684354560 | bytes 4194304 | tf_op jit(solution)/shard_map/blocks_4_5/pallas_call | solution.py:144
  74.3 7.2 %collective-permute-start.8 = (bf16[256,512]{1,0:T(8,128)(2,1)S(1)}, bf16[256,512]{1,0:T(8,128)(2,1)S(1)}, u32[]{:S(2)}, u32[]{:S(2)}) collective-permute-start(bf16[256,512]{1,0:T(8,128)(2,1)S(1)} %get-tuple-element.25), channel_id=1, source_target_pairs={{0,504},{8,0},{16,8},{24,16},{32,24},{40,32},{48,40},{56,48},{64,5... | collective-permute-start | bytes 786440 | tf_op jit(solution)/shard_map/ppermute | solution.py:17
  81.6 1.9 %collective-permute-start.12 = (bf16[256,512]{1,0:T(8,128)(2,1)S(1)}, bf16[256,512]{1,0:T(8,128)(2,1)S(1)}, u32[]{:S(2)}, u32[]{:S(2)}) collective-permute-start(bf16[256,512]{1,0:T(8,128)(2,1)S(1)} %get-tuple-element.29), channel_id=1, source_target_pairs={{0,8},{8,16},{16,24},{24,32},{32,40},{40,48},{48,56},{56,64},{64,7... | collective-permute-start | bytes 786440 | tf_op jit(solution)/shard_map/ppermute | solution.py:17
  83.5 1.9 %collective-permute-done.8 = bf16[256,512]{1,0:T(8,128)(2,1)S(1)} collective-permute-done((bf16[256,512]{1,0:T(8,128)(2,1)S(1)}, bf16[256,512]{1,0:T(8,128)(2,1)S(1)}, u32[]{:S(2)}, u32[]{:S(2)}) %collective-permute-start.8) | collective-permute-done | bytes 262176 | tf_op jit(solution)/shard_map/ppermute | solution.py:17
  85.5 7.7 %collective-permute-start.9 = (bf16[256,512]{1,0:T(8,128)(2,1)S(1)}, bf16[256,512]{1,0:T(8,128)(2,1)S(1)}, u32[]{:S(2)}, u32[]{:S(2)}) collective-permute-start(bf16[256,512]{1,0:T(8,128)(2,1)S(1)} %add_convert_fusion.5), channel_id=1, source_target_pairs={{0,504},{8,0},{16,8},{24,16},{32,24},{40,32},{48,40},{56,48},{64,5... | collective-permute-start | bytes 786440 | tf_op jit(solution)/shard_map/ppermute | solution.py:17
  93.3 1.9 %collective-permute-start.13 = (bf16[256,512]{1,0:T(8,128)(2,1)S(1)}, bf16[256,512]{1,0:T(8,128)(2,1)S(1)}, u32[]{:S(2)}, u32[]{:S(2)}) collective-permute-start(bf16[256,512]{1,0:T(8,128)(2,1)S(1)} %add_convert_fusion.2), channel_id=1, source_target_pairs={{0,8},{8,16},{16,24},{24,32},{32,40},{40,48},{48,56},{56,64},{64,7... | collective-permute-start | bytes 786440 | tf_op jit(solution)/shard_map/ppermute | solution.py:17
  95.2 1.9 %collective-permute-done.9 = bf16[256,512]{1,0:T(8,128)(2,1)S(1)} collective-permute-done((bf16[256,512]{1,0:T(8,128)(2,1)S(1)}, bf16[256,512]{1,0:T(8,128)(2,1)S(1)}, u32[]{:S(2)}, u32[]{:S(2)}) %collective-permute-start.9) | collective-permute-done | bytes 262176 | tf_op jit(solution)/shard_map/ppermute | solution.py:17
  97.2 7.7 %collective-permute-start.10 = (bf16[256,512]{1,0:T(8,128)(2,1)S(1)}, bf16[256,512]{1,0:T(8,128)(2,1)S(1)}, u32[]{:S(2)}, u32[]{:S(2)}) collective-permute-start(bf16[256,512]{1,0:T(8,128)(2,1)S(1)} %add_convert_fusion.4), channel_id=1, source_target_pairs={{0,504},{8,0},{16,8},{24,16},{32,24},{40,32},{48,40},{56,48},{64,5... | collective-permute-start | bytes 786440 | tf_op jit(solution)/shard_map/ppermute | solution.py:17
  105.0 1.9 %collective-permute-start.14 = (bf16[256,512]{1,0:T(8,128)(2,1)S(1)}, bf16[256,512]{1,0:T(8,128)(2,1)S(1)}, u32[]{:S(2)}, u32[]{:S(2)}) collective-permute-start(bf16[256,512]{1,0:T(8,128)(2,1)S(1)} %add_convert_fusion.1), channel_id=1, source_target_pairs={{0,8},{8,16},{16,24},{24,32},{32,40},{40,48},{48,56},{56,64},{64,7... | collective-permute-start | bytes 786440 | tf_op jit(solution)/shard_map/ppermute | solution.py:17
  106.9 1.9 %collective-permute-done.10 = bf16[256,512]{1,0:T(8,128)(2,1)S(1)} collective-permute-done((bf16[256,512]{1,0:T(8,128)(2,1)S(1)}, bf16[256,512]{1,0:T(8,128)(2,1)S(1)}, u32[]{:S(2)}, u32[]{:S(2)}) %collective-permute-start.10) | collective-permute-done | bytes 262176 | tf_op jit(solution)/shard_map/ppermute | solution.py:17
  108.8 7.7 %collective-permute-start.11 = (bf16[256,512]{1,0:T(8,128)(2,1)S(1)}, bf16[256,512]{1,0:T(8,128)(2,1)S(1)}, u32[]{:S(2)}, u32[]{:S(2)}) collective-permute-start(bf16[256,512]{1,0:T(8,128)(2,1)S(1)} %add_convert_fusion.3), channel_id=1, source_target_pairs={{0,504},{8,0},{16,8},{24,16},{32,24},{40,32},{48,40},{56,48},{64,5... | collective-permute-start | bytes 786440 | tf_op jit(solution)/shard_map/ppermute | solution.py:17
  116.6 1.9 %collective-permute-start.15 = (bf16[256,512]{1,0:T(8,128)(2,1)S(1)}, bf16[256,512]{1,0:T(8,128)(2,1)S(1)}, u32[]{:S(2)}, u32[]{:S(2)}) collective-permute-start(bf16[256,512]{1,0:T(8,128)(2,1)S(1)} %add_convert_fusion), channel_id=1, source_target_pairs={{0,448},{8,456},{16,464},{24,472},{32,480},{40,488},{48,496},{56,5... | collective-permute-start | bytes 786440 | tf_op jit(solution)/shard_map/ppermute | solution.py:17
  118.5 1.1 turn_query_gradient.1
  120.4 4.4 %collective-permute-done.15 = bf16[256,512]{1,0:T(8,128)(2,1)S(1)} collective-permute-done((bf16[256,512]{1,0:T(8,128)(2,1)S(1)}, bf16[256,512]{1,0:T(8,128)(2,1)S(1)}, u32[]{:S(2)}, u32[]{:S(2)}) %collective-permute-start.15) | collective-permute-done | bytes 262176 | tf_op jit(solution)/shard_map/ppermute | solution.py:17
  (29 shorter events, 2.7 us)
Async XLA Ops:
  0.6 40.2 %copy-start = (bf16[256,1024]{1,0:T(8,128)(2,1)S(1)}, bf16[256,1024]{1,0:T(8,128)(2,1)}, u32[]{:S(2)}) copy-start(bf16[256,1024]{1,0:T(8,128)(2,1)} %o.1) | copy-start | bytes 1572868
  2.5 38.3 %copy-start.4 = (f32[8,256]{1,0:T(8,128)S(1)}, f32[8,256]{1,0:T(8,128)}, u32[]{:S(2)}) copy-start(f32[8,256]{1,0:T(8,128)} %lse.9) | copy-start | bytes 24580
  2.5 22.9 %collective-permute-start.4 = (bf16[256,512]{1,0:T(8,128)(2,1)S(1)}, bf16[256,512]{1,0:T(8,128)(2,1)S(1)}, u32[]{:S(2)}, u32[]{:S(2)}) collective-permute-start(bf16[256,512]{1,0:T(8,128)(2,1)S(1)} %constant_dynamic-update-slice_fusion.kv), channel_id=1, source_target_pairs={{0,64},{8,72},{16,80},{24,88},{32,96},{40,104},{48,112},{56,120},{... | collective-permute-start | bytes 786440 | tf_op jit(solution)/shard_map/ppermute | solution.py:17
  6.8 20.5 %collective-permute-start = (bf16[256,512]{1,0:T(8,128)(2,1)S(1)}, bf16[256,512]{1,0:T(8,128)(2,1)S(1)}, u32[]{:S(2)}, u32[]{:S(2)}) collective-permute-start(bf16[256,512]{1,0:T(8,128)(2,1)S(1)} %constant_dynamic-update-slice_fusion.kv), channel_id=1, source_target_pairs={{0,8},{8,16},{16,24},{24,32},{32,40},{40,48},{48,56},{56,64},{64,7... | collective-permute-start | bytes 786440 | tf_op jit(solution)/shard_map/ppermute | solution.py:17
  25.4 9.1 %collective-permute-start.5 = (bf16[256,512]{1,0:T(8,128)(2,1)S(1)}, bf16[256,512]{1,0:T(8,128)(2,1)S(1)}, u32[]{:S(2)}, u32[]{:S(2)}) collective-permute-start(bf16[256,512]{1,0:T(8,128)(2,1)S(1)} %collective-permute-done.4.kv_b), channel_id=1, source_target_pairs={{0,504},{8,0},{16,8},{24,16},{32,24},{40,32},{48,40},{56,48},{64,5... | collective-permute-start | bytes 786440 | tf_op jit(solution)/shard_map/ppermute | solution.py:17
  27.3 11.6 %collective-permute-start.1 = (bf16[256,512]{1,0:T(8,128)(2,1)S(1)}, bf16[256,512]{1,0:T(8,128)(2,1)S(1)}, u32[]{:S(2)}, u32[]{:S(2)}) collective-permute-start(bf16[256,512]{1,0:T(8,128)(2,1)S(1)} %collective-permute-done.kv_a), channel_id=1, source_target_pairs={{0,8},{8,16},{16,24},{24,32},{32,40},{40,48},{48,56},{56,64},{64,7... | collective-permute-start | bytes 786440 | tf_op jit(solution)/shard_map/ppermute | solution.py:17
  31.3 9.6 %copy-start.5 = (s32[16]{0:T(128)S(1)}, s32[16]{0:T(128)}, u32[]{:S(2)}) copy-start(s32[16]{0:T(128)} %lengths.9) | copy-start | bytes 196
  34.5 16.2 %collective-permute-start.6 = (bf16[256,512]{1,0:T(8,128)(2,1)S(1)}, bf16[256,512]{1,0:T(8,128)(2,1)S(1)}, u32[]{:S(2)}, u32[]{:S(2)}) collective-permute-start(bf16[256,512]{1,0:T(8,128)(2,1)S(1)} %collective-permute-done.5.kv_b), channel_id=1, source_target_pairs={{0,504},{8,0},{16,8},{24,16},{32,24},{40,32},{48,40},{56,48},{64,5... | collective-permute-start | bytes 786440 | tf_op jit(solution)/shard_map/ppermute | solution.py:17
  38.9 19.0 %collective-permute-start.2 = (bf16[256,512]{1,0:T(8,128)(2,1)S(1)}, bf16[256,512]{1,0:T(8,128)(2,1)S(1)}, u32[]{:S(2)}, u32[]{:S(2)}) collective-permute-start(bf16[256,512]{1,0:T(8,128)(2,1)S(1)} %collective-permute-done.1.kv_a), channel_id=1, source_target_pairs={{0,8},{8,16},{16,24},{24,32},{32,40},{40,48},{48,56},{56,64},{64,7... | collective-permute-start | bytes 786440 | tf_op jit(solution)/shard_map/ppermute | solution.py:17
  40.9 1.0 copy-start.1
  41.9 1.0 copy-start.2
  43.0 2.9 %copy-start.3 = (bf16[256,1024]{1,0:T(8,128)(2,1)S(1)}, bf16[256,1024]{1,0:T(8,128)(2,1)}, u32[]{:S(2)}) copy-start(bf16[256,1024]{1,0:T(8,128)(2,1)} %do.9) | copy-start | bytes 1572868
  50.7 18.9 %collective-permute-start.7 = (bf16[256,512]{1,0:T(8,128)(2,1)S(1)}, bf16[256,512]{1,0:T(8,128)(2,1)S(1)}, u32[]{:S(2)}, u32[]{:S(2)}) collective-permute-start(bf16[256,512]{1,0:T(8,128)(2,1)S(1)} %collective-permute-done.6.kv_b), channel_id=1, source_target_pairs={{0,504},{8,0},{16,8},{24,16},{32,24},{40,32},{48,40},{56,48},{64,5... | collective-permute-start | bytes 786440 | tf_op jit(solution)/shard_map/ppermute | solution.py:17
  57.9 11.6 %collective-permute-start.3 = (bf16[256,512]{1,0:T(8,128)(2,1)S(1)}, bf16[256,512]{1,0:T(8,128)(2,1)S(1)}, u32[]{:S(2)}, u32[]{:S(2)}) collective-permute-start(bf16[256,512]{1,0:T(8,128)(2,1)S(1)} %collective-permute-done.2.kv_a), channel_id=1, source_target_pairs={{0,8},{8,16},{16,24},{24,32},{32,40},{40,48},{48,56},{56,64},{64,7... | collective-permute-start | bytes 786440 | tf_op jit(solution)/shard_map/ppermute | solution.py:17
  74.3 11.1 %collective-permute-start.8 = (bf16[256,512]{1,0:T(8,128)(2,1)S(1)}, bf16[256,512]{1,0:T(8,128)(2,1)S(1)}, u32[]{:S(2)}, u32[]{:S(2)}) collective-permute-start(bf16[256,512]{1,0:T(8,128)(2,1)S(1)} %get-tuple-element.25), channel_id=1, source_target_pairs={{0,504},{8,0},{16,8},{24,16},{32,24},{40,32},{48,40},{56,48},{64,5... | collective-permute-start | bytes 786440 | tf_op jit(solution)/shard_map/ppermute | solution.py:17
  81.6 11.7 %collective-permute-start.12 = (bf16[256,512]{1,0:T(8,128)(2,1)S(1)}, bf16[256,512]{1,0:T(8,128)(2,1)S(1)}, u32[]{:S(2)}, u32[]{:S(2)}) collective-permute-start(bf16[256,512]{1,0:T(8,128)(2,1)S(1)} %get-tuple-element.29), channel_id=1, source_target_pairs={{0,8},{8,16},{16,24},{24,32},{32,40},{40,48},{48,56},{56,64},{64,7... | collective-permute-start | bytes 786440 | tf_op jit(solution)/shard_map/ppermute | solution.py:17
  85.5 11.6 %collective-permute-start.9 = (bf16[256,512]{1,0:T(8,128)(2,1)S(1)}, bf16[256,512]{1,0:T(8,128)(2,1)S(1)}, u32[]{:S(2)}, u32[]{:S(2)}) collective-permute-start(bf16[256,512]{1,0:T(8,128)(2,1)S(1)} %add_convert_fusion.5), channel_id=1, source_target_pairs={{0,504},{8,0},{16,8},{24,16},{32,24},{40,32},{48,40},{56,48},{64,5... | collective-permute-start | bytes 786440 | tf_op jit(solution)/shard_map/ppermute | solution.py:17
  93.3 11.6 %collective-permute-start.13 = (bf16[256,512]{1,0:T(8,128)(2,1)S(1)}, bf16[256,512]{1,0:T(8,128)(2,1)S(1)}, u32[]{:S(2)}, u32[]{:S(2)}) collective-permute-start(bf16[256,512]{1,0:T(8,128)(2,1)S(1)} %add_convert_fusion.2), channel_id=1, source_target_pairs={{0,8},{8,16},{16,24},{24,32},{32,40},{40,48},{48,56},{56,64},{64,7... | collective-permute-start | bytes 786440 | tf_op jit(solution)/shard_map/ppermute | solution.py:17
  97.2 11.6 %collective-permute-start.10 = (bf16[256,512]{1,0:T(8,128)(2,1)S(1)}, bf16[256,512]{1,0:T(8,128)(2,1)S(1)}, u32[]{:S(2)}, u32[]{:S(2)}) collective-permute-start(bf16[256,512]{1,0:T(8,128)(2,1)S(1)} %add_convert_fusion.4), channel_id=1, source_target_pairs={{0,504},{8,0},{16,8},{24,16},{32,24},{40,32},{48,40},{56,48},{64,5... | collective-permute-start | bytes 786440 | tf_op jit(solution)/shard_map/ppermute | solution.py:17
  105.0 11.6 %collective-permute-start.14 = (bf16[256,512]{1,0:T(8,128)(2,1)S(1)}, bf16[256,512]{1,0:T(8,128)(2,1)S(1)}, u32[]{:S(2)}, u32[]{:S(2)}) collective-permute-start(bf16[256,512]{1,0:T(8,128)(2,1)S(1)} %add_convert_fusion.1), channel_id=1, source_target_pairs={{0,8},{8,16},{16,24},{24,32},{32,40},{40,48},{48,56},{56,64},{64,7... | collective-permute-start | bytes 786440 | tf_op jit(solution)/shard_map/ppermute | solution.py:17
  108.8 11.6 %collective-permute-start.11 = (bf16[256,512]{1,0:T(8,128)(2,1)S(1)}, bf16[256,512]{1,0:T(8,128)(2,1)S(1)}, u32[]{:S(2)}, u32[]{:S(2)}) collective-permute-start(bf16[256,512]{1,0:T(8,128)(2,1)S(1)} %add_convert_fusion.3), channel_id=1, source_target_pairs={{0,504},{8,0},{16,8},{24,16},{32,24},{40,32},{48,40},{56,48},{64,5... | collective-permute-start | bytes 786440 | tf_op jit(solution)/shard_map/ppermute | solution.py:17
  116.6 8.3 %collective-permute-start.15 = (bf16[256,512]{1,0:T(8,128)(2,1)S(1)}, bf16[256,512]{1,0:T(8,128)(2,1)S(1)}, u32[]{:S(2)}, u32[]{:S(2)}) collective-permute-start(bf16[256,512]{1,0:T(8,128)(2,1)S(1)} %add_convert_fusion), channel_id=1, source_target_pairs={{0,448},{8,456},{16,464},{24,472},{32,480},{40,488},{48,496},{56,5... | collective-permute-start | bytes 786440 | tf_op jit(solution)/shard_map/ppermute | solution.py:17

commit v2 on v1

v2 whole, which is shorter than its diff:
```python
import functools
import math

import jax
import jax.numpy as jnp
from jax import lax
from jax.experimental import pallas as pl
from jax.experimental.pallas import tpu as pltpu
from jax.sharding import PartitionSpec as P

HEAD_WIDTH = 128
LOG2_E = math.log2(math.e)


def moved(array, by):
    count = lax.axis_size("ctx")
    return lax.ppermute(array, "ctx", [(i, (i + by) % count) for i in range(count)])


def doc_starts(index_ref, lengths_ref, rows):
    first = index_ref[0] * rows
    places = first + lax.broadcasted_iota(jnp.int32, (1, rows), 1)
    start = jnp.zeros((1, rows), jnp.int32)
    end = jnp.int32(0)
    for doc in range(lengths_ref.shape[0]):
        end = end + lengths_ref[doc]
        start = jnp.where(places >= end, end, start)
    return start - first


def transposed_dot(a, b):
    return lax.dot_general(a, b, (((1,), (1,)), ((), ())), preferred_element_type=jnp.float32)


def one_block(distance, starts, q, do, lse, delta, kv, dq, dkv):
    rows, width = q.shape[0], HEAD_WIDTH
    groups = kv.shape[1] // (2 * width)
    per_group = q.shape[1] // (groups * width)
    key = lax.broadcasted_iota(jnp.int32, (rows, rows), 0)
    live = key - distance * rows >= starts
    if distance == 0:
        live &= key <= lax.broadcasted_iota(jnp.int32, (rows, rows), 1)
    scale = LOG2_E * width**-0.5

    def group_heads(group):
        return [pl.ds(h * width, width) for h in range(group * per_group, (group + 1) * per_group)]

    held = []
    for group in range(groups):
        k = kv[:, pl.ds(group * width, width)]
        v = kv[:, pl.ds((groups + group) * width, width)]
        probs, dscores = [], []
        for n, columns in enumerate(group_heads(group)):
            head = pl.ds(group * per_group + n, 1)
            score = transposed_dot(k, q[:, columns]) * scale - lse[head, :] * LOG2_E
            prob = jnp.where(live, jnp.exp2(score), 0.0)
            dscore = prob * (transposed_dot(v, do[:, columns]) - delta[head, :])
            probs.append(prob.astype(jnp.bfloat16))
            dscores.append(dscore.astype(jnp.bfloat16))
        held.append((jnp.concatenate(probs, axis=1), jnp.concatenate(dscores, axis=1), k.T))
    for group, (prob, dscore, k_t) in enumerate(held):
        dq_group = jnp.dot(k_t, dscore, preferred_element_type=jnp.float32)
        for n, columns in enumerate(group_heads(group)):
            dq_head = dq_group[:, n * rows : (n + 1) * rows]
            if distance == 0:
                dq[columns, :] = dq_head
            else:
                dq[columns, :] += dq_head
        q_rows = jnp.concatenate([q[:, columns] for columns in group_heads(group)], axis=0)
        do_rows = jnp.concatenate([do[:, columns] for columns in group_heads(group)], axis=0)
        dk = jnp.dot(dscore, q_rows, preferred_element_type=jnp.float32)
        dv = jnp.dot(prob, do_rows, preferred_element_type=jnp.float32)
        dkv[:, pl.ds(group * width, width)] = dk.astype(dkv.dtype)
        dkv[:, pl.ds((groups + group) * width, width)] = dv.astype(dkv.dtype)


def join_kernel(keys, values, kv, sems):
    width = keys.shape[1]
    copies = [
        pltpu.make_async_copy(keys, kv.at[:, pl.ds(0, width)], sems.at[0]),
        pltpu.make_async_copy(values, kv.at[:, pl.ds(width, width)], sems.at[1]),
    ]
    for copy in copies:
        copy.start()
    for copy in copies:
        copy.wait()


def own_kernel(index, lengths, q, do, o, lse, kv, dq, dkv, delta, starts):
    rows, heads = q.shape[0], lse.shape[0]
    lane = lax.broadcasted_iota(jnp.int32, (rows, HEAD_WIDTH), 1)
    sums = jnp.zeros((rows, HEAD_WIDTH), jnp.float32)
    for head in range(heads):
        columns = pl.ds(head * HEAD_WIDTH, HEAD_WIDTH)
        product = do[:, columns].astype(jnp.float32) * o[:, columns].astype(jnp.float32)
        sums = jnp.where(lane == head, jnp.sum(product, axis=1, keepdims=True), sums)
    delta[...] = sums.T[:heads]
    starts[...] = doc_starts(index, lengths, rows)
    one_block(0, starts[...], q, do, lse, delta, kv, dq, dkv)


def block_kernel(distance, starts, q, do, lse, delta, kv, dq_in, dq, dkv):
    del dq_in
    one_block(distance, starts[...], q, do, lse, delta, kv, dq, dkv)


def turn_kernel(dq_t, dq):
    for head in range(dq.shape[1] // HEAD_WIDTH):
        columns = pl.ds(head * HEAD_WIDTH, HEAD_WIDTH)
        dq[:, columns] = (dq_t[columns, :].T * HEAD_WIDTH**-0.5).astype(dq.dtype)


def total_kernel(own, *refs):
    *parts, key_gradient, value_gradient = refs
    split = key_gradient.shape[1]
    total = own[...]
    for part in parts:
        total += part[...].astype(jnp.float32)
    key_gradient[...] = (total[:, :split] * HEAD_WIDTH**-0.5).astype(key_gradient.dtype)
    value_gradient[...] = total[:, split:].astype(value_gradient.dtype)


VMEM = pl.BlockSpec(memory_space=pltpu.VMEM)
SMEM = pl.BlockSpec(memory_space=pltpu.SMEM)


def call(kernel, name, scalars, arrays, outs, flops, aliases=None):
    return pl.pallas_call(
        kernel,
        name=name,
        out_shape=outs,
        in_specs=[SMEM] * scalars + [VMEM] * arrays,
        out_specs=[VMEM] * len(outs),
        input_output_aliases=aliases or {},
        cost_estimate=pl.CostEstimate(flops=flops, bytes_accessed=3 << 20, transcendentals=flops // 1280),
        compiler_params=pltpu.CompilerParams(vmem_limit_bytes=32 << 20),
    )


def body(query, keys, values, output, output_gradient, row_log_norm, doc_lengths):
    rows, heads = query.shape[0], row_log_norm.shape[0]
    bf16, f32 = jnp.bfloat16, jnp.float32
    index = lax.axis_index("ctx").astype(jnp.int32).reshape(1)
    joined_shape = (rows, 2 * keys.shape[1])
    dq_shape = jax.ShapeDtypeStruct((query.shape[1], rows), f32)
    flops = 10 * heads * rows * rows * HEAD_WIDTH
    own_outs = [
        dq_shape,
        jax.ShapeDtypeStruct(joined_shape, f32),
        jax.ShapeDtypeStruct((heads, rows), f32),
        jax.ShapeDtypeStruct((1, rows), jnp.int32),
    ]

    kv = pl.pallas_call(
        join_kernel,
        name="keys_and_values",
        out_shape=jax.ShapeDtypeStruct(joined_shape, bf16),
        in_specs=[pl.BlockSpec(memory_space=pltpu.HBM)] * 2,
        out_specs=VMEM,
        scratch_shapes=[pltpu.SemaphoreType.DMA((2,))],
        cost_estimate=pl.CostEstimate(flops=0, bytes_accessed=1 << 19, transcendentals=0),
    )(keys, values)
    dq, own, delta, starts = call(own_kernel, "own_block", 2, 5, own_outs, flops)(
        index, doc_lengths, query, output_gradient, output, row_log_norm, kv
    )

    def block(distance, kv, dq):
        outs = [dq_shape, jax.ShapeDtypeStruct(joined_shape, bf16)]
        kernel = functools.partial(block_kernel, distance)
        return call(kernel, f"block_{distance}", 0, 7, outs, flops, {6: 0})(
            starts, query, output_gradient, row_log_norm, delta, kv, dq
        )

    def joined(*parts):
        return sum(part.astype(f32) for part in parts).astype(bf16)

    tie = lax.optimization_barrier
    got, part = {}, {}
    got[1], got[8] = moved(kv, 1), moved(kv, 8)
    for near in range(1, 4):
        far = 9 - near
        got[near], dq = tie((got[near], dq))
        got[near + 1] = moved(got[near], 1)
        dq, part[near] = block(near, got[near], dq)
        got[far], dq = tie((got[far], dq))
        got[far - 1] = moved(got[far], -1)
        dq, part[far] = block(far, got[far], dq)

    dq, part[4] = block(4, got[4], dq)
    near = moved(part[4], -1)
    dq, part[5] = block(5, got[5], dq)
    far = moved(part[5], 1)
    home = [moved(part[8], -8)]
    near = moved(joined(near, part[3]), -1)
    far = moved(joined(far, part[6]), 1)
    near = moved(joined(near, part[2]), -1)
    far = moved(joined(far, part[7]), -7)
    near = moved(joined(near, part[1]), -1)
    home += [near, far]
    (grad_query,) = call(turn_kernel, "turn_query_gradient", 0, 1, [jax.ShapeDtypeStruct(query.shape, bf16)], 0)(dq)
    half = jax.ShapeDtypeStruct(keys.shape, bf16)
    key_gradient, value_gradient = call(total_kernel, "total", 0, 1 + len(home), [half, half], 0)(own, *home)
    return grad_query, key_gradient, value_gradient


def solution(mesh):
    tokens = P(("dp", "ctx"), "head")
    return jax.shard_map(
        body,
        mesh=mesh,
        in_specs=(tokens,) * 5 + (P("head", ("dp", "ctx")), P("dp")),
        out_specs=(tokens,) * 3,
        check_vma=False,
    )
```

time: 127 us -> 107 us (0.84)
  waiting for transfers between devices: 29.2 us -> 15.4 us
  Pallas kernels: 23 us -> 17.7 us
    ppermute x16, waiting for transfers between devices: 29.2 us -> 15.4 us  [moved(): lax.ppermute(array, 'ctx', [(i, (i + by) % count) for i in range(count)])]
    pallas_call x5 -> x11, Pallas kernels: 21.9 us -> 16.6 us  [the longest x8 11.8 us: block(): call(kernel, f'block_{distance}', 0, 7, outs, flops, {6: 0})]
    unnamed x13 -> x16, local copies, waits for them, and re-layouts: 3.07 us -> 3.68 us
  transfers between devices with their start and end apart: 16 -> 16, of which waited for: 7 -> 8; matrix products, arithmetic and copies ran while one was open for 0% -> 0% of each run, Pallas kernels for 14% -> 14%
where the time goes in v2:
time: 107 us; the launch traced here: 105 us
  starting transfers between devices  67.1 us (63%)
  Pallas kernels  17.7 us (17%)
  waiting for transfers between devices  15.4 us (14%)
  local copies, waits for them, and re-layouts  3.68 us (3%)
    ppermute x16, starting transfers between devices, moved(): lax.ppermute(array, 'ctx', [(i, (i + by) % count) for i in range(count)])  67.1 us
    ppermute x16, waiting for transfers between devices, moved(): lax.ppermute(array, 'ctx', [(i, (i + by) % count) for i in range(count)])  15.4 us
    pallas_call x8, Pallas kernels, block(): call(kernel, f'block_{distance}', 0, 7, outs, flops, {6: 0})  11.8 us
    unnamed x16, local copies, waits for them, and re-layouts  3.68 us
    pallas_call x1, Pallas kernels, body(): call(own_kernel, 'own_block', 2, 5, own_outs, flops)  2.23 us
  transfers between devices with their start and end apart: 16, of which 8 were waited for; matrix products, arithmetic and copies ran while one was open for 0% of the time, Pallas kernels for 14%

profile of v2, /device:TPU:6, one launch (start us, length us, event | category | flops | bytes accessed | tf_op | source)
XLA Modules:
  0.0 105.2 jit_solution(16711175372852159673)
XLA Ops:
  0.6 1.7 %keys_and_values.1.kv = bf16[256,512]{1,0:T(8,128)(2,1)} custom-call(bf16[256,256]{1,0:T(8,128)(2,1)} %keys.1, bf16[256,256]{1,0:T(8,128)(2,1)} %values.1), custom_call_target="tpu_custom_call" | custom-call | bytes 524288 | tf_op jit(solution)/shard_map/keys_and_values/pallas_call | solution.py:154
  2.4 3.5 %collective-permute-start.1 = (bf16[256,512]{1,0:T(8,128)(2,1)}, bf16[256,512]{1,0:T(8,128)(2,1)S(1)}, u32[]{:S(2)}, u32[]{:S(2)}) collective-permute-start(bf16[256,512]{1,0:T(8,128)(2,1)} %keys_and_values.1.kv), channel_id=1, source_target_pairs={{0,8},{8,16},{16,24},{24,32},{32,40},{40,48},{48,56},{56,64},{64,7... | collective-permute-start | bytes 786440 | tf_op jit(solution)/shard_map/ppermute | solution.py:17
  5.9 4.3 %collective-permute-start = (bf16[256,512]{1,0:T(8,128)(2,1)}, bf16[256,512]{1,0:T(8,128)(2,1)S(1)}, u32[]{:S(2)}, u32[]{:S(2)}) collective-permute-start(bf16[256,512]{1,0:T(8,128)(2,1)} %keys_and_values.1.kv), channel_id=1, source_target_pairs={{0,64},{8,72},{16,80},{24,88},{32,96},{40,104},{48,112},{56,120},{... | collective-permute-start | bytes 786440 | tf_op jit(solution)/shard_map/ppermute | solution.py:17
  11.8 1.0 copy-done.2
  13.9 2.2 %own_block.1 = (f32[1024,256]{1,0:T(8,128)S(1)}, f32[256,512]{1,0:T(8,128)S(1)}, f32[8,256]{1,0:T(8,128)S(1)}, s32[1,256]{1,0:T(1,128)S(1)}) custom-call(s32[1]{0:T(128)} %bitcast.index, s32[16]{0:T(128)S(1)} %copy-done.7, bf16[256,1024]{1,0:T(8,128)(2,1)S(1)} %copy-done.2, bf16[256,1024]{1,0:T(8,128)(2,1)S(1)} %copy-done.4, ...), custom_call_target="tpu_custom_call" | custom-call | flops 671088640 | bytes 3145728 | tf_op jit(solution)/shard_map/own_block/pallas_call | solution.py:163
  16.1 6.7 %collective-permute-done.1.kv = bf16[256,512]{1,0:T(8,128)(2,1)S(1)} collective-permute-done((bf16[256,512]{1,0:T(8,128)(2,1)}, bf16[256,512]{1,0:T(8,128)(2,1)S(1)}, u32[]{:S(2)}, u32[]{:S(2)}) %collective-permute-start.1) | collective-permute-done | bytes 262176 | tf_op jit(solution)/shard_map/ppermute | solution.py:17
  22.9 1.9 %collective-permute-start.3 = (bf16[256,512]{1,0:T(8,128)(2,1)S(1)}, bf16[256,512]{1,0:T(8,128)(2,1)S(1)}, u32[]{:S(2)}, u32[]{:S(2)}) collective-permute-start(bf16[256,512]{1,0:T(8,128)(2,1)S(1)} %collective-permute-done.1.kv), channel_id=1, source_target_pairs={{0,8},{8,16},{16,24},{24,32},{32,40},{40,48},{48,56},{56,64},{64,7... | collective-permute-start | bytes 786440 | tf_op jit(solution)/shard_map/ppermute | solution.py:17
  24.8 1.5 %block_1.1 = (f32[1024,256]{1,0:T(8,128)S(1)}, bf16[256,512]{1,0:T(8,128)(2,1)S(1)}) custom-call(s32[1,256]{1,0:T(1,128)S(1)} %get-tuple-element.37.starts, bf16[256,1024]{1,0:T(8,128)(2,1)S(1)} %copy-done.2, bf16[256,1024]{1,0:T(8,128)(2,1)S(1)} %copy-done.4, f32[8,256]{1,0:T(8,128)S(1)} %copy-done.6, ...), custom_call_target="tpu_custom_call", output_to_operand_aliasing={{0}: (6, {})} | custom-call | flops 671088640 | bytes 3145728 | tf_op jit(solution)/shard_map/block_1/pallas_call | solution.py:170
  26.2 2.1 %collective-permute-done.kv = bf16[256,512]{1,0:T(8,128)(2,1)S(1)} collective-permute-done((bf16[256,512]{1,0:T(8,128)(2,1)}, bf16[256,512]{1,0:T(8,128)(2,1)S(1)}, u32[]{:S(2)}, u32[]{:S(2)}) %collective-permute-start) | collective-permute-done | bytes 262176 | tf_op jit(solution)/shard_map/ppermute | solution.py:17
  28.4 5.3 %collective-permute-start.2 = (bf16[256,512]{1,0:T(8,128)(2,1)S(1)}, bf16[256,512]{1,0:T(8,128)(2,1)S(1)}, u32[]{:S(2)}, u32[]{:S(2)}) collective-permute-start(bf16[256,512]{1,0:T(8,128)(2,1)S(1)} %collective-permute-done.kv), channel_id=1, source_target_pairs={{0,504},{8,0},{16,8},{24,16},{32,24},{40,32},{48,40},{56,48},{64,5... | collective-permute-start | bytes 786440 | tf_op jit(solution)/shard_map/ppermute | solution.py:17
  33.6 1.5 %block_8.1 = (f32[1024,256]{1,0:T(8,128)S(1)}, bf16[256,512]{1,0:T(8,128)(2,1)S(1)}) custom-call(s32[1,256]{1,0:T(1,128)S(1)} %get-tuple-element.37.starts, bf16[256,1024]{1,0:T(8,128)(2,1)S(1)} %copy-done.2, bf16[256,1024]{1,0:T(8,128)(2,1)S(1)} %copy-done.4, f32[8,256]{1,0:T(8,128)S(1)} %copy-done.6, ...), custom_call_target="tpu_custom_call", output_to_operand_aliasing={{0}: (6, {})} | custom-call | flops 671088640 | bytes 3145728 | tf_op jit(solution)/shard_map/block_8/pallas_call | solution.py:170
  35.5 1.9 %collective-permute-start.5 = (bf16[256,512]{1,0:T(8,128)(2,1)S(1)}, bf16[256,512]{1,0:T(8,128)(2,1)S(1)}, u32[]{:S(2)}, u32[]{:S(2)}) collective-permute-start(bf16[256,512]{1,0:T(8,128)(2,1)S(1)} %collective-permute-done.3.kv), channel_id=1, source_target_pairs={{0,8},{8,16},{16,24},{24,32},{32,40},{40,48},{48,56},{56,64},{64,7... | collective-permute-start | bytes 786440 | tf_op jit(solution)/shard_map/ppermute | solution.py:17
  37.4 1.5 %block_2.1 = (f32[1024,256]{1,0:T(8,128)S(1)}, bf16[256,512]{1,0:T(8,128)(2,1)S(1)}) custom-call(s32[1,256]{1,0:T(1,128)S(1)} %get-tuple-element.37.starts, bf16[256,1024]{1,0:T(8,128)(2,1)S(1)} %copy-done.3, bf16[256,1024]{1,0:T(8,128)(2,1)S(1)} %copy-done.4, f32[8,256]{1,0:T(8,128)S(1)} %copy-done.6, ...), custom_call_target="tpu_custom_call", output_to_operand_aliasing={{0}: (6, {})} | custom-call | flops 671088640 | bytes 3145728 | tf_op jit(solution)/shard_map/block_2/pallas_call | solution.py:170
  38.9 7.4 %collective-permute-start.4 = (bf16[256,512]{1,0:T(8,128)(2,1)S(1)}, bf16[256,512]{1,0:T(8,128)(2,1)S(1)}, u32[]{:S(2)}, u32[]{:S(2)}) collective-permute-start(bf16[256,512]{1,0:T(8,128)(2,1)S(1)} %collective-permute-done.2.kv), channel_id=1, source_target_pairs={{0,504},{8,0},{16,8},{24,16},{32,24},{40,32},{48,40},{56,48},{64,5... | collective-permute-start | bytes 786440 | tf_op jit(solution)/shard_map/ppermute | solution.py:17
  46.3 1.5 %block_7.1 = (f32[1024,256]{1,0:T(8,128)S(1)}, bf16[256,512]{1,0:T(8,128)(2,1)S(1)}) custom-call(s32[1,256]{1,0:T(1,128)S(1)} %get-tuple-element.37.starts, bf16[256,1024]{1,0:T(8,128)(2,1)S(1)} %copy-done.3, bf16[256,1024]{1,0:T(8,128)(2,1)S(1)} %copy-done.4, f32[8,256]{1,0:T(8,128)S(1)} %copy-done.6, ...), custom_call_target="tpu_custom_call", output_to_operand_aliasing={{0}: (6, {})} | custom-call | flops 671088640 | bytes 3145728 | tf_op jit(solution)/shard_map/block_7/pallas_call | solution.py:170
  47.8 1.9 %collective-permute-start.7 = (bf16[256,512]{1,0:T(8,128)(2,1)S(1)}, bf16[256,512]{1,0:T(8,128)(2,1)S(1)}, u32[]{:S(2)}, u32[]{:S(2)}) collective-permute-start(bf16[256,512]{1,0:T(8,128)(2,1)S(1)} %collective-permute-done.5.kv), channel_id=1, source_target_pairs={{0,8},{8,16},{16,24},{24,32},{32,40},{40,48},{48,56},{56,64},{64,7... | collective-permute-start | bytes 786440 | tf_op jit(solution)/shard_map/ppermute | solution.py:17
  49.8 1.5 %block_3.1 = (f32[1024,256]{1,0:T(8,128)S(1)}, bf16[256,512]{1,0:T(8,128)(2,1)S(1)}) custom-call(s32[1,256]{1,0:T(1,128)S(1)} %get-tuple-element.37.starts, bf16[256,1024]{1,0:T(8,128)(2,1)S(1)} %copy-done.3, bf16[256,1024]{1,0:T(8,128)(2,1)S(1)} %copy-done.5, f32[8,256]{1,0:T(8,128)S(1)} %copy-done.6, ...), custom_call_target="tpu_custom_call", output_to_operand_aliasing={{0}: (6, {})} | custom-call | flops 671088640 | bytes 3145728 | tf_op jit(solution)/shard_map/block_3/pallas_call | solution.py:170
  51.3 7.4 %collective-permute-start.6 = (bf16[256,512]{1,0:T(8,128)(2,1)S(1)}, bf16[256,512]{1,0:T(8,128)(2,1)S(1)}, u32[]{:S(2)}, u32[]{:S(2)}) collective-permute-start(bf16[256,512]{1,0:T(8,128)(2,1)S(1)} %collective-permute-done.4.kv), channel_id=1, source_target_pairs={{0,504},{8,0},{16,8},{24,16},{32,24},{40,32},{48,40},{56,48},{64,5... | collective-permute-start | bytes 786440 | tf_op jit(solution)/shard_map/ppermute | solution.py:17
  58.7 1.5 %block_6.1 = (f32[1024,256]{1,0:T(8,128)S(1)}, bf16[256,512]{1,0:T(8,128)(2,1)S(1)}) custom-call(s32[1,256]{1,0:T(1,128)S(1)} %get-tuple-element.37.starts, bf16[256,1024]{1,0:T(8,128)(2,1)S(1)} %copy-done.3, bf16[256,1024]{1,0:T(8,128)(2,1)S(1)} %copy-done.5, f32[8,256]{1,0:T(8,128)S(1)} %copy-done.6, ...), custom_call_target="tpu_custom_call", output_to_operand_aliasing={{0}: (6, {})} | custom-call | flops 671088640 | bytes 3145728 | tf_op jit(solution)/shard_map/block_6/pallas_call | solution.py:170
  60.2 1.5 %block_4.1 = (f32[1024,256]{1,0:T(8,128)S(1)}, bf16[256,512]{1,0:T(8,128)(2,1)S(1)}) custom-call(s32[1,256]{1,0:T(1,128)S(1)} %get-tuple-element.37.starts, bf16[256,1024]{1,0:T(8,128)(2,1)S(1)} %copy-done.3, bf16[256,1024]{1,0:T(8,128)(2,1)S(1)} %copy-done.5, f32[8,256]{1,0:T(8,128)S(1)} %copy-done.6, ...), custom_call_target="tpu_custom_call", output_to_operand_aliasing={{0}: (6, {})} | custom-call | flops 671088640 | bytes 3145728 | tf_op jit(solution)/shard_map/block_4/pallas_call | solution.py:170
  61.7 1.9 %collective-permute-start.9 = (bf16[256,512]{1,0:T(8,128)(2,1)S(1)}, bf16[256,512]{1,0:T(8,128)(2,1)S(1)}, u32[]{:S(2)}, u32[]{:S(2)}) collective-permute-start(bf16[256,512]{1,0:T(8,128)(2,1)S(1)} %get-tuple-element.62), channel_id=1, source_target_pairs={{0,504},{8,0},{16,8},{24,16},{32,24},{40,32},{48,40},{56,48},{64,5... | collective-permute-start | bytes 786440 | tf_op jit(solution)/shard_map/ppermute | solution.py:17
  63.6 1.5 %block_5.1 = (f32[1024,256]{1,0:T(8,128)S(1)}, bf16[256,512]{1,0:T(8,128)(2,1)S(1)}) custom-call(s32[1,256]{1,0:T(1,128)S(1)} %get-tuple-element.37.starts, bf16[256,1024]{1,0:T(8,128)(2,1)S(1)} %copy-done.3, bf16[256,1024]{1,0:T(8,128)(2,1)S(1)} %copy-done.5, f32[8,256]{1,0:T(8,128)S(1)} %copy-done.6, ...), custom_call_target="tpu_custom_call", output_to_operand_aliasing={{0}: (6, {})} | custom-call | flops 671088640 | bytes 3145728 | tf_op jit(solution)/shard_map/block_5/pallas_call | solution.py:170
  65.1 3.9 %collective-permute-start.13 = (bf16[256,512]{1,0:T(8,128)(2,1)S(1)}, bf16[256,512]{1,0:T(8,128)(2,1)S(1)}, u32[]{:S(2)}, u32[]{:S(2)}) collective-permute-start(bf16[256,512]{1,0:T(8,128)(2,1)S(1)} %get-tuple-element.66), channel_id=1, source_target_pairs={{0,8},{8,16},{16,24},{24,32},{32,40},{40,48},{48,56},{56,64},{64,7... | collective-permute-start | bytes 786440 | tf_op jit(solution)/shard_map/ppermute | solution.py:17
  70.0 5.8 %collective-permute-start.10 = (bf16[256,512]{1,0:T(8,128)(2,1)S(1)}, bf16[256,512]{1,0:T(8,128)(2,1)S(1)}, u32[]{:S(2)}, u32[]{:S(2)}) collective-permute-start(bf16[256,512]{1,0:T(8,128)(2,1)S(1)} %add_convert_fusion.4), channel_id=1, source_target_pairs={{0,504},{8,0},{16,8},{24,16},{32,24},{40,32},{48,40},{56,48},{64,5... | collective-permute-start | bytes 786440 | tf_op jit(solution)/shard_map/ppermute | solution.py:17
  75.8 1.3 %collective-permute-done.13 = bf16[256,512]{1,0:T(8,128)(2,1)S(1)} collective-permute-done((bf16[256,512]{1,0:T(8,128)(2,1)S(1)}, bf16[256,512]{1,0:T(8,128)(2,1)S(1)}, u32[]{:S(2)}, u32[]{:S(2)}) %collective-permute-start.13) | collective-permute-done | bytes 262176 | tf_op jit(solution)/shard_map/ppermute | solution.py:17
  77.2 1.9 %collective-permute-start.14 = (bf16[256,512]{1,0:T(8,128)(2,1)S(1)}, bf16[256,512]{1,0:T(8,128)(2,1)S(1)}, u32[]{:S(2)}, u32[]{:S(2)}) collective-permute-start(bf16[256,512]{1,0:T(8,128)(2,1)S(1)} %add_convert_fusion.1), channel_id=1, source_target_pairs={{0,8},{8,16},{16,24},{24,32},{32,40},{40,48},{48,56},{56,64},{64,7... | collective-permute-start | bytes 786440 | tf_op jit(solution)/shard_map/ppermute | solution.py:17
  79.7 7.7 %collective-permute-start.11 = (bf16[256,512]{1,0:T(8,128)(2,1)S(1)}, bf16[256,512]{1,0:T(8,128)(2,1)S(1)}, u32[]{:S(2)}, u32[]{:S(2)}) collective-permute-start(bf16[256,512]{1,0:T(8,128)(2,1)S(1)} %add_convert_fusion.3), channel_id=1, source_target_pairs={{0,504},{8,0},{16,8},{24,16},{32,24},{40,32},{48,40},{56,48},{64,5... | collective-permute-start | bytes 786440 | tf_op jit(solution)/shard_map/ppermute | solution.py:17
  87.5 1.9 %collective-permute-start.8 = (bf16[256,512]{1,0:T(8,128)(2,1)S(1)}, bf16[256,512]{1,0:T(8,128)(2,1)S(1)}, u32[]{:S(2)}, u32[]{:S(2)}) collective-permute-start(bf16[256,512]{1,0:T(8,128)(2,1)S(1)} %get-tuple-element.61), channel_id=1, source_target_pairs={{0,448},{8,456},{16,464},{24,472},{32,480},{40,488},{48,496},{56,5... | collective-permute-start | bytes 786440 | tf_op jit(solution)/shard_map/ppermute | solution.py:17
  89.5 1.9 %collective-permute-start.15 = (bf16[256,512]{1,0:T(8,128)(2,1)S(1)}, bf16[256,512]{1,0:T(8,128)(2,1)S(1)}, u32[]{:S(2)}, u32[]{:S(2)}) collective-permute-start(bf16[256,512]{1,0:T(8,128)(2,1)S(1)} %add_convert_fusion), channel_id=1, source_target_pairs={{0,456},{8,464},{16,472},{24,480},{32,488},{40,496},{48,504},{56,0... | collective-permute-start | bytes 786440 | tf_op jit(solution)/shard_map/ppermute | solution.py:17
  92.0 8.4 %collective-permute-start.12 = (bf16[256,512]{1,0:T(8,128)(2,1)S(1)}, bf16[256,512]{1,0:T(8,128)(2,1)S(1)}, u32[]{:S(2)}, u32[]{:S(2)}) collective-permute-start(bf16[256,512]{1,0:T(8,128)(2,1)S(1)} %add_convert_fusion.2), channel_id=1, source_target_pairs={{0,504},{8,0},{16,8},{24,16},{32,24},{40,32},{48,40},{56,48},{64,5... | collective-permute-start | bytes 786440 | tf_op jit(solution)/shard_map/ppermute | solution.py:17
  100.5 1.1 %turn_query_gradient.1 = bf16[256,1024]{1,0:T(8,128)(2,1)} custom-call(f32[1024,256]{1,0:T(8,128)S(1)} %get-tuple-element.59.dq_t), custom_call_target="tpu_custom_call" | custom-call | bytes 3145728 | tf_op jit(solution)/shard_map/turn_query_gradient/pallas_call | solution.py:200
  101.6 2.8 %collective-permute-done.12.refs_1_ = bf16[256,512]{1,0:T(8,128)(2,1)S(1)} collective-permute-done((bf16[256,512]{1,0:T(8,128)(2,1)S(1)}, bf16[256,512]{1,0:T(8,128)(2,1)S(1)}, u32[]{:S(2)}, u32[]{:S(2)}) %collective-permute-start.12) | collective-permute-done | bytes 262176 | tf_op jit(solution)/shard_map/ppermute | solution.py:17
  (33 shorter events, 6.2 us)
Async XLA Ops:
  0.6 9.6 %copy-start.1 = (bf16[256,1024]{1,0:T(8,128)(2,1)S(1)}, bf16[256,1024]{1,0:T(8,128)(2,1)}, u32[]{:S(2)}) copy-start(bf16[256,1024]{1,0:T(8,128)(2,1)} %o.1) | copy-start | bytes 1572868
  2.4 7.8 %copy-start.6 = (f32[8,256]{1,0:T(8,128)S(1)}, f32[8,256]{1,0:T(8,128)}, u32[]{:S(2)}) copy-start(f32[8,256]{1,0:T(8,128)} %lse.17) | copy-start | bytes 24580
  2.4 20.5 %collective-permute-start.1 = (bf16[256,512]{1,0:T(8,128)(2,1)}, bf16[256,512]{1,0:T(8,128)(2,1)S(1)}, u32[]{:S(2)}, u32[]{:S(2)}) collective-permute-start(bf16[256,512]{1,0:T(8,128)(2,1)} %keys_and_values.1.kv), channel_id=1, source_target_pairs={{0,8},{8,16},{16,24},{24,32},{32,40},{40,48},{48,56},{56,64},{64,7... | collective-permute-start | bytes 786440 | tf_op jit(solution)/shard_map/ppermute | solution.py:17
  5.9 22.5 %collective-permute-start = (bf16[256,512]{1,0:T(8,128)(2,1)}, bf16[256,512]{1,0:T(8,128)(2,1)S(1)}, u32[]{:S(2)}, u32[]{:S(2)}) collective-permute-start(bf16[256,512]{1,0:T(8,128)(2,1)} %keys_and_values.1.kv), channel_id=1, source_target_pairs={{0,64},{8,72},{16,80},{24,88},{32,96},{40,104},{48,112},{56,120},{... | collective-permute-start | bytes 786440 | tf_op jit(solution)/shard_map/ppermute | solution.py:17
  10.2 0.7 copy-start.7
  10.8 0.9 copy-start
  11.8 1.0 copy-start.2
  12.8 1.0 copy-start.4
  22.9 12.6 %collective-permute-start.3 = (bf16[256,512]{1,0:T(8,128)(2,1)S(1)}, bf16[256,512]{1,0:T(8,128)(2,1)S(1)}, u32[]{:S(2)}, u32[]{:S(2)}) collective-permute-start(bf16[256,512]{1,0:T(8,128)(2,1)S(1)} %collective-permute-done.1.kv), channel_id=1, source_target_pairs={{0,8},{8,16},{16,24},{24,32},{32,40},{40,48},{48,56},{56,64},{64,7... | collective-permute-start | bytes 786440 | tf_op jit(solution)/shard_map/ppermute | solution.py:17
  28.4 9.0 %copy-start.3 = (bf16[256,1024]{1,0:T(8,128)(2,1)S(1)}, bf16[256,1024]{1,0:T(8,128)(2,1)}, u32[]{:S(2)}) copy-start(bf16[256,1024]{1,0:T(8,128)(2,1)} %q.17) | copy-start | bytes 1572868
  28.4 10.5 %collective-permute-start.2 = (bf16[256,512]{1,0:T(8,128)(2,1)S(1)}, bf16[256,512]{1,0:T(8,128)(2,1)S(1)}, u32[]{:S(2)}, u32[]{:S(2)}) collective-permute-start(bf16[256,512]{1,0:T(8,128)(2,1)S(1)} %collective-permute-done.kv), channel_id=1, source_target_pairs={{0,504},{8,0},{16,8},{24,16},{32,24},{40,32},{48,40},{56,48},{64,5... | collective-permute-start | bytes 786440 | tf_op jit(solution)/shard_map/ppermute | solution.py:17
  35.5 12.3 %collective-permute-start.5 = (bf16[256,512]{1,0:T(8,128)(2,1)S(1)}, bf16[256,512]{1,0:T(8,128)(2,1)S(1)}, u32[]{:S(2)}, u32[]{:S(2)}) collective-permute-start(bf16[256,512]{1,0:T(8,128)(2,1)S(1)} %collective-permute-done.3.kv), channel_id=1, source_target_pairs={{0,8},{8,16},{16,24},{24,32},{32,40},{40,48},{48,56},{56,64},{64,7... | collective-permute-start | bytes 786440 | tf_op jit(solution)/shard_map/ppermute | solution.py:17
  38.9 10.8 %copy-start.5 = (bf16[256,1024]{1,0:T(8,128)(2,1)S(1)}, bf16[256,1024]{1,0:T(8,128)(2,1)}, u32[]{:S(2)}) copy-start(bf16[256,1024]{1,0:T(8,128)(2,1)} %do.17) | copy-start | bytes 1572868
  38.9 12.3 %collective-permute-start.4 = (bf16[256,512]{1,0:T(8,128)(2,1)S(1)}, bf16[256,512]{1,0:T(8,128)(2,1)S(1)}, u32[]{:S(2)}, u32[]{:S(2)}) collective-permute-start(bf16[256,512]{1,0:T(8,128)(2,1)S(1)} %collective-permute-done.2.kv), channel_id=1, source_target_pairs={{0,504},{8,0},{16,8},{24,16},{32,24},{40,32},{48,40},{56,48},{64,5... | collective-permute-start | bytes 786440 | tf_op jit(solution)/shard_map/ppermute | solution.py:17
  47.8 12.4 %collective-permute-start.7 = (bf16[256,512]{1,0:T(8,128)(2,1)S(1)}, bf16[256,512]{1,0:T(8,128)(2,1)S(1)}, u32[]{:S(2)}, u32[]{:S(2)}) collective-permute-start(bf16[256,512]{1,0:T(8,128)(2,1)S(1)} %collective-permute-done.5.kv), channel_id=1, source_target_pairs={{0,8},{8,16},{16,24},{24,32},{32,40},{40,48},{48,56},{56,64},{64,7... | collective-permute-start | bytes 786440 | tf_op jit(solution)/shard_map/ppermute | solution.py:17
  51.3 12.3 %collective-permute-start.6 = (bf16[256,512]{1,0:T(8,128)(2,1)S(1)}, bf16[256,512]{1,0:T(8,128)(2,1)S(1)}, u32[]{:S(2)}, u32[]{:S(2)}) collective-permute-start(bf16[256,512]{1,0:T(8,128)(2,1)S(1)} %collective-permute-done.4.kv), channel_id=1, source_target_pairs={{0,504},{8,0},{16,8},{24,16},{32,24},{40,32},{48,40},{56,48},{64,5... | collective-permute-start | bytes 786440 | tf_op jit(solution)/shard_map/ppermute | solution.py:17
  61.7 8.3 %collective-permute-start.9 = (bf16[256,512]{1,0:T(8,128)(2,1)S(1)}, bf16[256,512]{1,0:T(8,128)(2,1)S(1)}, u32[]{:S(2)}, u32[]{:S(2)}) collective-permute-start(bf16[256,512]{1,0:T(8,128)(2,1)S(1)} %get-tuple-element.62), channel_id=1, source_target_pairs={{0,504},{8,0},{16,8},{24,16},{32,24},{40,32},{48,40},{56,48},{64,5... | collective-permute-start | bytes 786440 | tf_op jit(solution)/shard_map/ppermute | solution.py:17
  65.1 12.0 %collective-permute-start.13 = (bf16[256,512]{1,0:T(8,128)(2,1)S(1)}, bf16[256,512]{1,0:T(8,128)(2,1)S(1)}, u32[]{:S(2)}, u32[]{:S(2)}) collective-permute-start(bf16[256,512]{1,0:T(8,128)(2,1)S(1)} %get-tuple-element.66), channel_id=1, source_target_pairs={{0,8},{8,16},{16,24},{24,32},{32,40},{40,48},{48,56},{56,64},{64,7... | collective-permute-start | bytes 786440 | tf_op jit(solution)/shard_map/ppermute | solution.py:17
  70.0 9.6 %collective-permute-start.10 = (bf16[256,512]{1,0:T(8,128)(2,1)S(1)}, bf16[256,512]{1,0:T(8,128)(2,1)S(1)}, u32[]{:S(2)}, u32[]{:S(2)}) collective-permute-start(bf16[256,512]{1,0:T(8,128)(2,1)S(1)} %add_convert_fusion.4), channel_id=1, source_target_pairs={{0,504},{8,0},{16,8},{24,16},{32,24},{40,32},{48,40},{56,48},{64,5... | collective-permute-start | bytes 786440 | tf_op jit(solution)/shard_map/ppermute | solution.py:17
  77.2 12.2 %collective-permute-start.14 = (bf16[256,512]{1,0:T(8,128)(2,1)S(1)}, bf16[256,512]{1,0:T(8,128)(2,1)S(1)}, u32[]{:S(2)}, u32[]{:S(2)}) collective-permute-start(bf16[256,512]{1,0:T(8,128)(2,1)S(1)} %add_convert_fusion.1), channel_id=1, source_target_pairs={{0,8},{8,16},{16,24},{24,32},{32,40},{40,48},{48,56},{56,64},{64,7... | collective-permute-start | bytes 786440 | tf_op jit(solution)/shard_map/ppermute | solution.py:17
  79.7 12.2 %collective-permute-start.11 = (bf16[256,512]{1,0:T(8,128)(2,1)S(1)}, bf16[256,512]{1,0:T(8,128)(2,1)S(1)}, u32[]{:S(2)}, u32[]{:S(2)}) collective-permute-start(bf16[256,512]{1,0:T(8,128)(2,1)S(1)} %add_convert_fusion.3), channel_id=1, source_target_pairs={{0,504},{8,0},{16,8},{24,16},{32,24},{40,32},{48,40},{56,48},{64,5... | collective-permute-start | bytes 786440 | tf_op jit(solution)/shard_map/ppermute | solution.py:17
  87.5 14.2 %collective-permute-start.8 = (bf16[256,512]{1,0:T(8,128)(2,1)S(1)}, bf16[256,512]{1,0:T(8,128)(2,1)S(1)}, u32[]{:S(2)}, u32[]{:S(2)}) collective-permute-start(bf16[256,512]{1,0:T(8,128)(2,1)S(1)} %get-tuple-element.61), channel_id=1, source_target_pairs={{0,448},{8,456},{16,464},{24,472},{32,480},{40,488},{48,496},{56,5... | collective-permute-start | bytes 786440 | tf_op jit(solution)/shard_map/ppermute | solution.py:17
  89.5 12.2 %collective-permute-start.15 = (bf16[256,512]{1,0:T(8,128)(2,1)S(1)}, bf16[256,512]{1,0:T(8,128)(2,1)S(1)}, u32[]{:S(2)}, u32[]{:S(2)}) collective-permute-start(bf16[256,512]{1,0:T(8,128)(2,1)S(1)} %add_convert_fusion), channel_id=1, source_target_pairs={{0,456},{8,464},{16,472},{24,480},{32,488},{40,496},{48,504},{56,0... | collective-permute-start | bytes 786440 | tf_op jit(solution)/shard_map/ppermute | solution.py:17
  92.0 12.4 %collective-permute-start.12 = (bf16[256,512]{1,0:T(8,128)(2,1)S(1)}, bf16[256,512]{1,0:T(8,128)(2,1)S(1)}, u32[]{:S(2)}, u32[]{:S(2)}) collective-permute-start(bf16[256,512]{1,0:T(8,128)(2,1)S(1)} %add_convert_fusion.2), channel_id=1, source_target_pairs={{0,504},{8,0},{16,8},{24,16},{32,24},{40,32},{48,40},{56,48},{64,5... | collective-permute-start | bytes 786440 | tf_op jit(solution)/shard_map/ppermute | solution.py:17

commit v3 on v2

--- a/solution.py
+++ b/solution.py
@@ -13,6 +13,11 @@
 
 
 def moved(array, by):
+    count = lax.axis_size("ctx")
+    return lax.ppermute(array, "ctx", [(i, i + by) for i in range(max(0, -by), min(count, count - by))])
+
+
+def turned(array, by):
     count = lax.axis_size("ctx")
     return lax.ppermute(array, "ctx", [(i, (i + by) % count) for i in range(count)])
 
@@ -32,7 +37,7 @@
     return lax.dot_general(a, b, (((1,), (1,)), ((), ())), preferred_element_type=jnp.float32)
 
 
-def one_block(distance, starts, q, do, lse, delta, kv, dq, dkv):
+def one_block(distance, starts, q, do, lse, delta, kv, dq_before, dq, dkv):
     rows, width = q.shape[0], HEAD_WIDTH
     groups = kv.shape[1] // (2 * width)
     per_group = q.shape[1] // (groups * width)
@@ -62,10 +67,7 @@
         dq_group = jnp.dot(k_t, dscore, preferred_element_type=jnp.float32)
         for n, columns in enumerate(group_heads(group)):
             dq_head = dq_group[:, n * rows : (n + 1) * rows]
-            if distance == 0:
-                dq[columns, :] = dq_head
-            else:
-                dq[columns, :] += dq_head
+            dq[columns, :] = dq_head if dq_before is None else dq_before[columns, :] + dq_head
         q_rows = jnp.concatenate([q[:, columns] for columns in group_heads(group)], axis=0)
         do_rows = jnp.concatenate([do[:, columns] for columns in group_heads(group)], axis=0)
         dk = jnp.dot(dscore, q_rows, preferred_element_type=jnp.float32)
@@ -96,12 +98,20 @@
         sums = jnp.where(lane == head, jnp.sum(product, axis=1, keepdims=True), sums)
     delta[...] = sums.T[:heads]
     starts[...] = doc_starts(index, lengths, rows)
-    one_block(0, starts[...], q, do, lse, delta, kv, dq, dkv)
-
-
-def block_kernel(distance, starts, q, do, lse, delta, kv, dq_in, dq, dkv):
-    del dq_in
-    one_block(distance, starts[...], q, do, lse, delta, kv, dq, dkv)
+    one_block(0, starts[...], q, do, lse, delta, kv, None, dq, dkv)
+
+
+def block_kernel(distance, starts, q, do, lse, delta, kv, dq_before, dq, dkv):
+    reached = jnp.min(starts[...]) < -(distance - 1) * q.shape[0]
+
+    @pl.when(reached)
+    def _():
+        one_block(distance, starts[...], q, do, lse, delta, kv, dq_before, dq, dkv)
+
+    @pl.when(jnp.logical_not(reached))
+    def _():
+        dq[...] = dq_before[...]
+        dkv[...] = jnp.zeros_like(dkv)
 
 
 def turn_kernel(dq_t, dq):
@@ -176,27 +186,28 @@
 
     tie = lax.optimization_barrier
     got, part = {}, {}
-    got[1], got[8] = moved(kv, 1), moved(kv, 8)
+    got[1], got[8] = moved(kv, 1), turned(kv, 8)
     for near in range(1, 4):
         far = 9 - near
         got[near], dq = tie((got[near], dq))
         got[near + 1] = moved(got[near], 1)
         dq, part[near] = block(near, got[near], dq)
         got[far], dq = tie((got[far], dq))
-        got[far - 1] = moved(got[far], -1)
-        dq, part[far] = block(far, got[far], dq)
+        got[far - 1] = turned(got[far], -1)
+        if near < 3:
+            dq, part[far] = block(far, got[far], dq)
 
     dq, part[4] = block(4, got[4], dq)
     near = moved(part[4], -1)
     dq, part[5] = block(5, got[5], dq)
-    far = moved(part[5], 1)
-    home = [moved(part[8], -8)]
-    near = moved(joined(near, part[3]), -1)
-    far = moved(joined(far, part[6]), 1)
-    near = moved(joined(near, part[2]), -1)
-    far = moved(joined(far, part[7]), -7)
-    near = moved(joined(near, part[1]), -1)
-    home += [near, far]
+    dq, part[6] = block(6, got[6], dq)
+    far, far_by = turned(part[5], 2), turned(part[6], 1)
+    near = moved(joined(near, part[3]), -2)
+    near_by = moved(part[2], -1)
+    far = turned(joined(far, far_by, part[7]), -7)
+    home = [far, moved(part[8], -8)]
+    near = moved(joined(near, near_by, part[1]), -1)
+    home += [near]
     (grad_query,) = call(turn_kernel, "turn_query_gradient", 0, 1, [jax.ShapeDtypeStruct(query.shape, bf16)], 0)(dq)
     half = jax.ShapeDtypeStruct(keys.shape, bf16)
     key_gradient, value_gradient = call(total_kernel, "total", 0, 1 + len(home), [half, half], 0)(own, *home)

time: 107 us -> 101 us (0.944)
  the two profiles are of different devices: /device:TPU:6 before, /device:TPU:252 now
where the time goes in v3:
time: 101 us; the launch traced here: 100 us
  starting transfers between devices  55.5 us (55%)
  waiting for transfers between devices  26.7 us (26%)
  Pallas kernels  13.2 us (13%)
  local copies, waits for them, and re-layouts  3.68 us (4%)
    ppermute x9, starting transfers between devices, moved(): lax.ppermute(array, 'ctx', [(i, i + by) for i in range(max(0, -by), min(c...  40.2 us
    ppermute x9, waiting for transfers between devices, moved(): lax.ppermute(array, 'ctx', [(i, i + by) for i in range(max(0, -by), min(c...  16.7 us
    ppermute x7, starting transfers between devices, turned(): lax.ppermute(array, 'ctx', [(i, (i + by) % count) for i in range(count)])  15.3 us
    ppermute x7, waiting for transfers between devices, turned(): lax.ppermute(array, 'ctx', [(i, (i + by) % count) for i in range(count)])  10 us
    pallas_call x8, Pallas kernels, block(): call(kernel, f'block_{distance}', 0, 7, outs, flops, {6: 0})  7.26 us
    unnamed x14, local copies, waits for them, and re-layouts  3.68 us
    pallas_call x1, Pallas kernels, body(): call(own_kernel, 'own_block', 2, 5, own_outs, flops)  2.23 us
  transfers between devices with their start and end apart: 16, of which 7 were waited for; matrix products, arithmetic and copies ran while one was open for 0% of the time, Pallas kernels for 11%

profile of v3, /device:TPU:252, one launch (start us, length us, event | category | flops | bytes accessed | tf_op | source)
XLA Modules:
  0.0 100.2 jit_solution(4050827388935907334)
XLA Ops:
  0.6 1.7 %keys_and_values.1.kv = bf16[256,512]{1,0:T(8,128)(2,1)} custom-call(bf16[256,256]{1,0:T(8,128)(2,1)} %keys.1, bf16[256,256]{1,0:T(8,128)(2,1)} %values.1), custom_call_target="tpu_custom_call" | custom-call | bytes 524288 | tf_op jit(solution)/shard_map/keys_and_values/pallas_call | solution.py:164
  2.4 4.7 %collective-permute-start.1 = (bf16[256,512]{1,0:T(8,128)(2,1)}, bf16[256,512]{1,0:T(8,128)(2,1)S(1)}, u32[]{:S(2)}, u32[]{:S(2)}) collective-permute-start(bf16[256,512]{1,0:T(8,128)(2,1)} %keys_and_values.1.kv), channel_id=1, source_target_pairs={{0,8},{8,16},{16,24},{24,32},{32,40},{40,48},{48,56},{56,64},{64,7... | collective-permute-start | bytes 786440 | tf_op jit(solution)/shard_map/ppermute | solution.py:17
  7.1 3.4 %collective-permute-start = (bf16[256,512]{1,0:T(8,128)(2,1)}, bf16[256,512]{1,0:T(8,128)(2,1)S(1)}, u32[]{:S(2)}, u32[]{:S(2)}) collective-permute-start(bf16[256,512]{1,0:T(8,128)(2,1)} %keys_and_values.1.kv), channel_id=1, source_target_pairs={{0,64},{8,72},{16,80},{24,88},{32,96},{40,104},{48,112},{56,120},{... | collective-permute-start | bytes 786440 | tf_op jit(solution)/shard_map/ppermute | solution.py:22
  11.2 0.9 copy-done
  12.1 1.0 %copy-done.2 = bf16[256,1024]{1,0:T(8,128)(2,1)S(1)} copy-done((bf16[256,1024]{1,0:T(8,128)(2,1)S(1)}, bf16[256,1024]{1,0:T(8,128)(2,1)}, u32[]{:S(2)}) %copy-start.2) | copy-done | bytes 524312
  13.2 1.0 %copy-done.4 = bf16[256,1024]{1,0:T(8,128)(2,1)S(1)} copy-done((bf16[256,1024]{1,0:T(8,128)(2,1)S(1)}, bf16[256,1024]{1,0:T(8,128)(2,1)}, u32[]{:S(2)}) %copy-start.4) | copy-done | bytes 524312
  14.2 2.2 %own_block.1 = (f32[1024,256]{1,0:T(8,128)S(1)}, f32[256,512]{1,0:T(8,128)S(1)}, f32[8,256]{1,0:T(8,128)S(1)}, s32[1,256]{1,0:T(1,128)S(1)}) custom-call(s32[1]{0:T(128)} %bitcast.index, s32[16]{0:T(128)S(1)} %copy-done.6, bf16[256,1024]{1,0:T(8,128)(2,1)S(1)} %copy-done.2, bf16[256,1024]{1,0:T(8,128)(2,1)S(1)} %copy-done.4, ...), custom_call_target="tpu_custom_call" | custom-call | flops 671088640 | bytes 3145728 | tf_op jit(solution)/shard_map/own_block/pallas_call | solution.py:173
  16.4 4.2 %collective-permute-start.3 = (bf16[256,512]{1,0:T(8,128)(2,1)S(1)}, bf16[256,512]{1,0:T(8,128)(2,1)S(1)}, u32[]{:S(2)}, u32[]{:S(2)}) collective-permute-start(bf16[256,512]{1,0:T(8,128)(2,1)S(1)} %collective-permute-done.1.kv), channel_id=1, source_target_pairs={{0,8},{8,16},{16,24},{24,32},{32,40},{40,48},{48,56},{56,64},{64,7... | collective-permute-start | bytes 786440 | tf_op jit(solution)/shard_map/ppermute | solution.py:17
  20.7 1.8 %block_1.1 = (f32[1024,256]{1,0:T(8,128)S(1)}, bf16[256,512]{1,0:T(8,128)(2,1)S(1)}) custom-call(s32[1,256]{1,0:T(1,128)S(1)} %get-tuple-element.37.starts, bf16[256,1024]{1,0:T(8,128)(2,1)S(1)} %copy-done.2, bf16[256,1024]{1,0:T(8,128)(2,1)S(1)} %copy-done.4, f32[8,256]{1,0:T(8,128)S(1)} %copy-done.5, ...), custom_call_target="tpu_custom_call", output_to_operand_aliasing={{0}: (6, {})} | custom-call | flops 671088640 | bytes 3145728 | tf_op jit(solution)/shard_map/block_1/pallas_call | solution.py:180
  22.4 1.9 %collective-permute-start.2 = (bf16[256,512]{1,0:T(8,128)(2,1)S(1)}, bf16[256,512]{1,0:T(8,128)(2,1)S(1)}, u32[]{:S(2)}, u32[]{:S(2)}) collective-permute-start(bf16[256,512]{1,0:T(8,128)(2,1)S(1)} %collective-permute-done.kv), channel_id=1, source_target_pairs={{0,504},{8,0},{16,8},{24,16},{32,24},{40,32},{48,40},{56,48},{64,5... | collective-permute-start | bytes 786440 | tf_op jit(solution)/shard_map/ppermute | solution.py:22
  24.7 1.1 %collective-permute-done.3.kv = bf16[256,512]{1,0:T(8,128)(2,1)S(1)} collective-permute-done((bf16[256,512]{1,0:T(8,128)(2,1)S(1)}, bf16[256,512]{1,0:T(8,128)(2,1)S(1)}, u32[]{:S(2)}, u32[]{:S(2)}) %collective-permute-start.3) | collective-permute-done | bytes 262176 | tf_op jit(solution)/shard_map/ppermute | solution.py:17
  25.8 7.2 %collective-permute-start.5 = (bf16[256,512]{1,0:T(8,128)(2,1)S(1)}, bf16[256,512]{1,0:T(8,128)(2,1)S(1)}, u32[]{:S(2)}, u32[]{:S(2)}) collective-permute-start(bf16[256,512]{1,0:T(8,128)(2,1)S(1)} %collective-permute-done.3.kv), channel_id=1, source_target_pairs={{0,8},{8,16},{16,24},{24,32},{32,40},{40,48},{48,56},{56,64},{64,7... | collective-permute-start | bytes 786440 | tf_op jit(solution)/shard_map/ppermute | solution.py:17
  33.0 1.8 %block_2.1 = (f32[1024,256]{1,0:T(8,128)S(1)}, bf16[256,512]{1,0:T(8,128)(2,1)S(1)}) custom-call(s32[1,256]{1,0:T(1,128)S(1)} %get-tuple-element.37.starts, bf16[256,1024]{1,0:T(8,128)(2,1)S(1)} %copy-done.2, bf16[256,1024]{1,0:T(8,128)(2,1)S(1)} %copy-done.4, f32[8,256]{1,0:T(8,128)S(1)} %copy-done.5, ...), custom_call_target="tpu_custom_call", output_to_operand_aliasing={{0}: (6, {})} | custom-call | flops 671088640 | bytes 3145728 | tf_op jit(solution)/shard_map/block_2/pallas_call | solution.py:180
  34.8 2.1 %collective-permute-start.4 = (bf16[256,512]{1,0:T(8,128)(2,1)S(1)}, bf16[256,512]{1,0:T(8,128)(2,1)S(1)}, u32[]{:S(2)}, u32[]{:S(2)}) collective-permute-start(bf16[256,512]{1,0:T(8,128)(2,1)S(1)} %collective-permute-done.2.kv), channel_id=1, source_target_pairs={{0,504},{8,0},{16,8},{24,16},{32,24},{40,32},{48,40},{56,48},{64,5... | collective-permute-start | bytes 786440 | tf_op jit(solution)/shard_map/ppermute | solution.py:22
  37.2 7.3 %collective-permute-start.7 = (bf16[256,512]{1,0:T(8,128)(2,1)S(1)}, bf16[256,512]{1,0:T(8,128)(2,1)S(1)}, u32[]{:S(2)}, u32[]{:S(2)}) collective-permute-start(bf16[256,512]{1,0:T(8,128)(2,1)S(1)} %collective-permute-done.5.kv), channel_id=1, source_target_pairs={{0,8},{8,16},{16,24},{24,32},{32,40},{40,48},{48,56},{56,64},{64,7... | collective-permute-start | bytes 786440 | tf_op jit(solution)/shard_map/ppermute | solution.py:17
  44.6 1.8 %block_3.1 = (f32[1024,256]{1,0:T(8,128)S(1)}, bf16[256,512]{1,0:T(8,128)(2,1)S(1)}) custom-call(s32[1,256]{1,0:T(1,128)S(1)} %get-tuple-element.37.starts, bf16[256,1024]{1,0:T(8,128)(2,1)S(1)} %copy-done.3, bf16[256,1024]{1,0:T(8,128)(2,1)S(1)} %copy-done.4, f32[8,256]{1,0:T(8,128)S(1)} %copy-done.5, ...), custom_call_target="tpu_custom_call", output_to_operand_aliasing={{0}: (6, {})} | custom-call | flops 671088640 | bytes 3145728 | tf_op jit(solution)/shard_map/block_3/pallas_call | solution.py:180
  46.5 1.9 %collective-permute-start.6 = (bf16[256,512]{1,0:T(8,128)(2,1)S(1)}, bf16[256,512]{1,0:T(8,128)(2,1)S(1)}, u32[]{:S(2)}, u32[]{:S(2)}) collective-permute-start(bf16[256,512]{1,0:T(8,128)(2,1)S(1)} %collective-permute-done.4.kv), channel_id=1, source_target_pairs={{0,504},{8,0},{16,8},{24,16},{32,24},{40,32},{48,40},{56,48},{64,5... | collective-permute-start | bytes 786440 | tf_op jit(solution)/shard_map/ppermute | solution.py:22
  49.0 1.9 %collective-permute-start.12 = (bf16[256,512]{1,0:T(8,128)(2,1)S(1)}, bf16[256,512]{1,0:T(8,128)(2,1)S(1)}, u32[]{:S(2)}, u32[]{:S(2)}) collective-permute-start(bf16[256,512]{1,0:T(8,128)(2,1)S(1)} %get-tuple-element.65), channel_id=1, source_target_pairs={{8,0},{16,8},{24,16},{32,24},{40,32},{48,40},{56,48},{64,56},{72,6... | collective-permute-start | bytes 786440 | tf_op jit(solution)/shard_map/ppermute | solution.py:17
  50.9 9.9 %collective-permute-done.6.kv = bf16[256,512]{1,0:T(8,128)(2,1)S(1)} collective-permute-done((bf16[256,512]{1,0:T(8,128)(2,1)S(1)}, bf16[256,512]{1,0:T(8,128)(2,1)S(1)}, u32[]{:S(2)}, u32[]{:S(2)}) %collective-permute-start.6) | collective-permute-done | bytes 262176 | tf_op jit(solution)/shard_map/ppermute | solution.py:22
  61.5 1.9 %collective-permute-start.9 = (bf16[256,512]{1,0:T(8,128)(2,1)S(1)}, bf16[256,512]{1,0:T(8,128)(2,1)S(1)}, u32[]{:S(2)}, u32[]{:S(2)}) collective-permute-start(bf16[256,512]{1,0:T(8,128)(2,1)S(1)} %get-tuple-element.62), channel_id=1, source_target_pairs={{0,8},{8,16},{16,24},{24,32},{32,40},{40,48},{48,56},{56,64},{64,7... | collective-permute-start | bytes 786440 | tf_op jit(solution)/shard_map/ppermute | solution.py:22
  63.4 2.2 %collective-permute-start.8 = (bf16[256,512]{1,0:T(8,128)(2,1)S(1)}, bf16[256,512]{1,0:T(8,128)(2,1)S(1)}, u32[]{:S(2)}, u32[]{:S(2)}) collective-permute-start(bf16[256,512]{1,0:T(8,128)(2,1)S(1)} %get-tuple-element.61), channel_id=1, source_target_pairs={{0,16},{8,24},{16,32},{24,40},{32,48},{40,56},{48,64},{56,72},{64,... | collective-permute-start | bytes 786440 | tf_op jit(solution)/shard_map/ppermute | solution.py:22
  65.6 3.9 %collective-permute-start.14 = (bf16[256,512]{1,0:T(8,128)(2,1)S(1)}, bf16[256,512]{1,0:T(8,128)(2,1)S(1)}, u32[]{:S(2)}, u32[]{:S(2)}) collective-permute-start(bf16[256,512]{1,0:T(8,128)(2,1)S(1)} %get-tuple-element.67), channel_id=1, source_target_pairs={{8,0},{16,8},{24,16},{32,24},{40,32},{48,40},{56,48},{64,56},{72,6... | collective-permute-start | bytes 786440 | tf_op jit(solution)/shard_map/ppermute | solution.py:17
  69.6 4.6 %collective-permute-start.13 = (bf16[256,512]{1,0:T(8,128)(2,1)S(1)}, bf16[256,512]{1,0:T(8,128)(2,1)S(1)}, u32[]{:S(2)}, u32[]{:S(2)}) collective-permute-start(bf16[256,512]{1,0:T(8,128)(2,1)S(1)} %add_convert_fusion.1), channel_id=1, source_target_pairs={{16,0},{24,8},{32,16},{40,24},{48,32},{56,40},{64,48},{72,56},{80,... | collective-permute-start | bytes 786440 | tf_op jit(solution)/shard_map/ppermute | solution.py:17
  74.2 1.9 %collective-permute-start.11 = (bf16[256,512]{1,0:T(8,128)(2,1)S(1)}, bf16[256,512]{1,0:T(8,128)(2,1)S(1)}, u32[]{:S(2)}, u32[]{:S(2)}) collective-permute-start(bf16[256,512]{1,0:T(8,128)(2,1)S(1)} %get-tuple-element.64), channel_id=1, source_target_pairs={{64,0},{72,8},{80,16},{88,24},{96,32},{104,40},{112,48},{120,56},{... | collective-permute-start | bytes 786440 | tf_op jit(solution)/shard_map/ppermute | solution.py:17
  76.2 1.9 %collective-permute-start.10 = (bf16[256,512]{1,0:T(8,128)(2,1)S(1)}, bf16[256,512]{1,0:T(8,128)(2,1)S(1)}, u32[]{:S(2)}, u32[]{:S(2)}) collective-permute-start(bf16[256,512]{1,0:T(8,128)(2,1)S(1)} %add_convert_fusion.2), channel_id=1, source_target_pairs={{0,456},{8,464},{16,472},{24,480},{32,488},{40,496},{48,504},{56,0... | collective-permute-start | bytes 786440 | tf_op jit(solution)/shard_map/ppermute | solution.py:22
  78.2 5.6 %collective-permute-done.14 = bf16[256,512]{1,0:T(8,128)(2,1)S(1)} collective-permute-done((bf16[256,512]{1,0:T(8,128)(2,1)S(1)}, bf16[256,512]{1,0:T(8,128)(2,1)S(1)}, u32[]{:S(2)}, u32[]{:S(2)}) %collective-permute-start.14) | collective-permute-done | bytes 262176 | tf_op jit(solution)/shard_map/ppermute | solution.py:17
  83.7 4.0 %collective-permute-done.13 = bf16[256,512]{1,0:T(8,128)(2,1)S(1)} collective-permute-done((bf16[256,512]{1,0:T(8,128)(2,1)S(1)}, bf16[256,512]{1,0:T(8,128)(2,1)S(1)}, u32[]{:S(2)}, u32[]{:S(2)}) %collective-permute-start.13) | collective-permute-done | bytes 262176 | tf_op jit(solution)/shard_map/ppermute | solution.py:17
  87.8 4.4 %collective-permute-start.15 = (bf16[256,512]{1,0:T(8,128)(2,1)S(1)}, bf16[256,512]{1,0:T(8,128)(2,1)S(1)}, u32[]{:S(2)}, u32[]{:S(2)}) collective-permute-start(bf16[256,512]{1,0:T(8,128)(2,1)S(1)} %add_convert_fusion), channel_id=1, source_target_pairs={{8,0},{16,8},{24,16},{32,24},{40,32},{48,40},{56,48},{64,56},{72,6... | collective-permute-start | bytes 786440 | tf_op jit(solution)/shard_map/ppermute | solution.py:17
  92.3 1.1 %turn_query_gradient.1 = bf16[256,1024]{1,0:T(8,128)(2,1)} custom-call(f32[1024,256]{1,0:T(8,128)S(1)} %get-tuple-element.59.dq_t), custom_call_target="tpu_custom_call" | custom-call | bytes 3145728 | tf_op jit(solution)/shard_map/turn_query_gradient/pallas_call | solution.py:211
  93.4 1.4 %collective-permute-done.11.refs_1_ = bf16[256,512]{1,0:T(8,128)(2,1)S(1)} collective-permute-done((bf16[256,512]{1,0:T(8,128)(2,1)S(1)}, bf16[256,512]{1,0:T(8,128)(2,1)S(1)}, u32[]{:S(2)}, u32[]{:S(2)}) %collective-permute-start.11) | collective-permute-done | bytes 262176 | tf_op jit(solution)/shard_map/ppermute | solution.py:17
  94.8 4.6 %collective-permute-done.15.refs_2_ = bf16[256,512]{1,0:T(8,128)(2,1)S(1)} collective-permute-done((bf16[256,512]{1,0:T(8,128)(2,1)S(1)}, bf16[256,512]{1,0:T(8,128)(2,1)S(1)}, u32[]{:S(2)}, u32[]{:S(2)}) %collective-permute-start.15) | collective-permute-done | bytes 262176 | tf_op jit(solution)/shard_map/ppermute | solution.py:17
  99.4 0.8 total.1
  (29 shorter events, 3.1 us)
Async XLA Ops:
  0.6 9.9 %copy-start.1 = (bf16[256,1024]{1,0:T(8,128)(2,1)S(1)}, bf16[256,1024]{1,0:T(8,128)(2,1)}, u32[]{:S(2)}) copy-start(bf16[256,1024]{1,0:T(8,128)(2,1)} %o.1) | copy-start | bytes 1572868
  2.4 8.1 %copy-start.5 = (f32[8,256]{1,0:T(8,128)S(1)}, f32[8,256]{1,0:T(8,128)}, u32[]{:S(2)}) copy-start(f32[8,256]{1,0:T(8,128)} %lse.17) | copy-start | bytes 24580
  2.4 14.0 %collective-permute-start.1 = (bf16[256,512]{1,0:T(8,128)(2,1)}, bf16[256,512]{1,0:T(8,128)(2,1)S(1)}, u32[]{:S(2)}, u32[]{:S(2)}) collective-permute-start(bf16[256,512]{1,0:T(8,128)(2,1)} %keys_and_values.1.kv), channel_id=1, source_target_pairs={{0,8},{8,16},{16,24},{24,32},{32,40},{40,48},{48,56},{56,64},{64,7... | collective-permute-start | bytes 786440 | tf_op jit(solution)/shard_map/ppermute | solution.py:17
  7.1 15.3 %collective-permute-start = (bf16[256,512]{1,0:T(8,128)(2,1)}, bf16[256,512]{1,0:T(8,128)(2,1)S(1)}, u32[]{:S(2)}, u32[]{:S(2)}) collective-permute-start(bf16[256,512]{1,0:T(8,128)(2,1)} %keys_and_values.1.kv), channel_id=1, source_target_pairs={{0,64},{8,72},{16,80},{24,88},{32,96},{40,104},{48,112},{56,120},{... | collective-permute-start | bytes 786440 | tf_op jit(solution)/shard_map/ppermute | solution.py:22
  10.5 0.7 copy-start.6
  11.2 0.9 copy-start
  12.1 1.0 %copy-start.2 = (bf16[256,1024]{1,0:T(8,128)(2,1)S(1)}, bf16[256,1024]{1,0:T(8,128)(2,1)}, u32[]{:S(2)}) copy-start(bf16[256,1024]{1,0:T(8,128)(2,1)} %q.17) | copy-start | bytes 1572868
  13.2 1.0 %copy-start.4 = (bf16[256,1024]{1,0:T(8,128)(2,1)S(1)}, bf16[256,1024]{1,0:T(8,128)(2,1)}, u32[]{:S(2)}) copy-start(bf16[256,1024]{1,0:T(8,128)(2,1)} %do.17) | copy-start | bytes 1572868
  16.4 9.4 %collective-permute-start.3 = (bf16[256,512]{1,0:T(8,128)(2,1)S(1)}, bf16[256,512]{1,0:T(8,128)(2,1)S(1)}, u32[]{:S(2)}, u32[]{:S(2)}) collective-permute-start(bf16[256,512]{1,0:T(8,128)(2,1)S(1)} %collective-permute-done.1.kv), channel_id=1, source_target_pairs={{0,8},{8,16},{16,24},{24,32},{32,40},{40,48},{48,56},{56,64},{64,7... | collective-permute-start | bytes 786440 | tf_op jit(solution)/shard_map/ppermute | solution.py:17
  22.4 12.3 %collective-permute-start.2 = (bf16[256,512]{1,0:T(8,128)(2,1)S(1)}, bf16[256,512]{1,0:T(8,128)(2,1)S(1)}, u32[]{:S(2)}, u32[]{:S(2)}) collective-permute-start(bf16[256,512]{1,0:T(8,128)(2,1)S(1)} %collective-permute-done.kv), channel_id=1, source_target_pairs={{0,504},{8,0},{16,8},{24,16},{32,24},{40,32},{48,40},{56,48},{64,5... | collective-permute-start | bytes 786440 | tf_op jit(solution)/shard_map/ppermute | solution.py:22
  25.8 11.4 %collective-permute-start.5 = (bf16[256,512]{1,0:T(8,128)(2,1)S(1)}, bf16[256,512]{1,0:T(8,128)(2,1)S(1)}, u32[]{:S(2)}, u32[]{:S(2)}) collective-permute-start(bf16[256,512]{1,0:T(8,128)(2,1)S(1)} %collective-permute-done.3.kv), channel_id=1, source_target_pairs={{0,8},{8,16},{16,24},{24,32},{32,40},{40,48},{48,56},{56,64},{64,7... | collective-permute-start | bytes 786440 | tf_op jit(solution)/shard_map/ppermute | solution.py:17
  34.8 9.8 %copy-start.3 = (bf16[256,1024]{1,0:T(8,128)(2,1)S(1)}, bf16[256,1024]{1,0:T(8,128)(2,1)}, u32[]{:S(2)}) copy-start(bf16[256,1024]{1,0:T(8,128)(2,1)} %q.17) | copy-start | bytes 1572868
  34.8 11.7 %collective-permute-start.4 = (bf16[256,512]{1,0:T(8,128)(2,1)S(1)}, bf16[256,512]{1,0:T(8,128)(2,1)S(1)}, u32[]{:S(2)}, u32[]{:S(2)}) collective-permute-start(bf16[256,512]{1,0:T(8,128)(2,1)S(1)} %collective-permute-done.2.kv), channel_id=1, source_target_pairs={{0,504},{8,0},{16,8},{24,16},{32,24},{40,32},{48,40},{56,48},{64,5... | collective-permute-start | bytes 786440 | tf_op jit(solution)/shard_map/ppermute | solution.py:22
  37.2 11.2 %collective-permute-start.7 = (bf16[256,512]{1,0:T(8,128)(2,1)S(1)}, bf16[256,512]{1,0:T(8,128)(2,1)S(1)}, u32[]{:S(2)}, u32[]{:S(2)}) collective-permute-start(bf16[256,512]{1,0:T(8,128)(2,1)S(1)} %collective-permute-done.5.kv), channel_id=1, source_target_pairs={{0,8},{8,16},{16,24},{24,32},{32,40},{40,48},{48,56},{56,64},{64,7... | collective-permute-start | bytes 786440 | tf_op jit(solution)/shard_map/ppermute | solution.py:17
  46.5 14.3 %collective-permute-start.6 = (bf16[256,512]{1,0:T(8,128)(2,1)S(1)}, bf16[256,512]{1,0:T(8,128)(2,1)S(1)}, u32[]{:S(2)}, u32[]{:S(2)}) collective-permute-start(bf16[256,512]{1,0:T(8,128)(2,1)S(1)} %collective-permute-done.4.kv), channel_id=1, source_target_pairs={{0,504},{8,0},{16,8},{24,16},{32,24},{40,32},{48,40},{56,48},{64,5... | collective-permute-start | bytes 786440 | tf_op jit(solution)/shard_map/ppermute | solution.py:22
  49.0 20.6 %collective-permute-start.12 = (bf16[256,512]{1,0:T(8,128)(2,1)S(1)}, bf16[256,512]{1,0:T(8,128)(2,1)S(1)}, u32[]{:S(2)}, u32[]{:S(2)}) collective-permute-start(bf16[256,512]{1,0:T(8,128)(2,1)S(1)} %get-tuple-element.65), channel_id=1, source_target_pairs={{8,0},{16,8},{24,16},{32,24},{40,32},{48,40},{56,48},{64,56},{72,6... | collective-permute-start | bytes 786440 | tf_op jit(solution)/shard_map/ppermute | solution.py:17
  61.5 14.6 %collective-permute-start.9 = (bf16[256,512]{1,0:T(8,128)(2,1)S(1)}, bf16[256,512]{1,0:T(8,128)(2,1)S(1)}, u32[]{:S(2)}, u32[]{:S(2)}) collective-permute-start(bf16[256,512]{1,0:T(8,128)(2,1)S(1)} %get-tuple-element.62), channel_id=1, source_target_pairs={{0,8},{8,16},{16,24},{24,32},{32,40},{40,48},{48,56},{56,64},{64,7... | collective-permute-start | bytes 786440 | tf_op jit(solution)/shard_map/ppermute | solution.py:22
  63.4 12.7 %collective-permute-start.8 = (bf16[256,512]{1,0:T(8,128)(2,1)S(1)}, bf16[256,512]{1,0:T(8,128)(2,1)S(1)}, u32[]{:S(2)}, u32[]{:S(2)}) collective-permute-start(bf16[256,512]{1,0:T(8,128)(2,1)S(1)} %get-tuple-element.61), channel_id=1, source_target_pairs={{0,16},{8,24},{16,32},{24,40},{32,48},{40,56},{48,64},{56,72},{64,... | collective-permute-start | bytes 786440 | tf_op jit(solution)/shard_map/ppermute | solution.py:22
  65.6 18.1 %collective-permute-start.14 = (bf16[256,512]{1,0:T(8,128)(2,1)S(1)}, bf16[256,512]{1,0:T(8,128)(2,1)S(1)}, u32[]{:S(2)}, u32[]{:S(2)}) collective-permute-start(bf16[256,512]{1,0:T(8,128)(2,1)S(1)} %get-tuple-element.67), channel_id=1, source_target_pairs={{8,0},{16,8},{24,16},{32,24},{40,32},{48,40},{56,48},{64,56},{72,6... | collective-permute-start | bytes 786440 | tf_op jit(solution)/shard_map/ppermute | solution.py:17
  69.6 18.1 %collective-permute-start.13 = (bf16[256,512]{1,0:T(8,128)(2,1)S(1)}, bf16[256,512]{1,0:T(8,128)(2,1)S(1)}, u32[]{:S(2)}, u32[]{:S(2)}) collective-permute-start(bf16[256,512]{1,0:T(8,128)(2,1)S(1)} %add_convert_fusion.1), channel_id=1, source_target_pairs={{16,0},{24,8},{32,16},{40,24},{48,32},{56,40},{64,48},{72,56},{80,... | collective-permute-start | bytes 786440 | tf_op jit(solution)/shard_map/ppermute | solution.py:17
  74.2 20.6 %collective-permute-start.11 = (bf16[256,512]{1,0:T(8,128)(2,1)S(1)}, bf16[256,512]{1,0:T(8,128)(2,1)S(1)}, u32[]{:S(2)}, u32[]{:S(2)}) collective-permute-start(bf16[256,512]{1,0:T(8,128)(2,1)S(1)} %get-tuple-element.64), channel_id=1, source_target_pairs={{64,0},{72,8},{80,16},{88,24},{96,32},{104,40},{112,48},{120,56},{... | collective-permute-start | bytes 786440 | tf_op jit(solution)/shard_map/ppermute | solution.py:17
  76.2 18.5 %collective-permute-start.10 = (bf16[256,512]{1,0:T(8,128)(2,1)S(1)}, bf16[256,512]{1,0:T(8,128)(2,1)S(1)}, u32[]{:S(2)}, u32[]{:S(2)}) collective-permute-start(bf16[256,512]{1,0:T(8,128)(2,1)S(1)} %add_convert_fusion.2), channel_id=1, source_target_pairs={{0,456},{8,464},{16,472},{24,480},{32,488},{40,496},{48,504},{56,0... | collective-permute-start | bytes 786440 | tf_op jit(solution)/shard_map/ppermute | solution.py:22
  87.8 11.6 %collective-permute-start.15 = (bf16[256,512]{1,0:T(8,128)(2,1)S(1)}, bf16[256,512]{1,0:T(8,128)(2,1)S(1)}, u32[]{:S(2)}, u32[]{:S(2)}) collective-permute-start(bf16[256,512]{1,0:T(8,128)(2,1)S(1)} %add_convert_fusion), channel_id=1, source_target_pairs={{8,0},{16,8},{24,16},{32,24},{40,32},{48,40},{56,48},{64,56},{72,6... | collective-permute-start | bytes 786440 | tf_op jit(solution)/shard_map/ppermute | solution.py:17

commit v4 on v3

--- a/solution.py
+++ b/solution.py
@@ -102,7 +102,7 @@
 
 
 def block_kernel(distance, starts, q, do, lse, delta, kv, dq_before, dq, dkv):
-    reached = jnp.min(starts[...]) < -(distance - 1) * q.shape[0]
+    reached = starts[...][0, 0] < -(distance - 1) * q.shape[0]
 
     @pl.when(reached)
     def _():
@@ -199,9 +199,10 @@
 
     dq, part[4] = block(4, got[4], dq)
     near = moved(part[4], -1)
+    dq, part[6] = block(6, got[6], dq)
+    far_by = turned(part[6], 1)
     dq, part[5] = block(5, got[5], dq)
-    dq, part[6] = block(6, got[6], dq)
-    far, far_by = turned(part[5], 2), turned(part[6], 1)
+    far = turned(part[5], 2)
     near = moved(joined(near, part[3]), -2)
     near_by = moved(part[2], -1)
     far = turned(joined(far, far_by, part[7]), -7)

time: 101 us -> 101 us (level)
  the two profiles are of different devices: /device:TPU:252 before, /device:TPU:250 now
where the time goes in v4:
time: 101 us; the launch traced here: 99.7 us
  starting transfers between devices  56.1 us (56%)
  waiting for transfers between devices  21.1 us (21%)
  Pallas kernels  17.6 us (17%)
  local copies, waits for them, and re-layouts  3.68 us (4%)
    ppermute x9, starting transfers between devices, moved(): lax.ppermute(array, 'ctx', [(i, i + by) for i in range(max(0, -by), min(c...  41.1 us
    ppermute x7, starting transfers between devices, turned(): lax.ppermute(array, 'ctx', [(i, (i + by) % count) for i in range(count)])  15 us
    ppermute x9, waiting for transfers between devices, moved(): lax.ppermute(array, 'ctx', [(i, i + by) for i in range(max(0, -by), min(c...  14.5 us
    pallas_call x8, Pallas kernels, block(): call(kernel, f'block_{distance}', 0, 7, outs, flops, {6: 0})  11.7 us
    ppermute x7, waiting for transfers between devices, turned(): lax.ppermute(array, 'ctx', [(i, (i + by) % count) for i in range(count)])  6.58 us
    unnamed x14, local copies, waits for them, and re-layouts  3.68 us
    pallas_call x1, Pallas kernels, body(): call(own_kernel, 'own_block', 2, 5, own_outs, flops)  2.23 us
  transfers between devices with their start and end apart: 16, of which 8 were waited for; matrix products, arithmetic and copies ran while one was open for 0% of the time, Pallas kernels for 15%

profile of v4, /device:TPU:250, one launch (start us, length us, event | category | flops | bytes accessed | tf_op | source)
XLA Modules:
  0.0 99.7 jit_solution(515358714619671239)
XLA Ops:
  0.6 1.7 %keys_and_values.1.kv = bf16[256,512]{1,0:T(8,128)(2,1)} custom-call(bf16[256,256]{1,0:T(8,128)(2,1)} %keys.1, bf16[256,256]{1,0:T(8,128)(2,1)} %values.1), custom_call_target="tpu_custom_call" | custom-call | bytes 524288 | tf_op jit(solution)/shard_map/keys_and_values/pallas_call | solution.py:164
  2.4 4.7 %collective-permute-start.1 = (bf16[256,512]{1,0:T(8,128)(2,1)}, bf16[256,512]{1,0:T(8,128)(2,1)S(1)}, u32[]{:S(2)}, u32[]{:S(2)}) collective-permute-start(bf16[256,512]{1,0:T(8,128)(2,1)} %keys_and_values.1.kv), channel_id=1, source_target_pairs={{0,8},{8,16},{16,24},{24,32},{32,40},{40,48},{48,56},{56,64},{64,7... | collective-permute-start | bytes 786440 | tf_op jit(solution)/shard_map/ppermute | solution.py:17
  7.1 3.4 %collective-permute-start = (bf16[256,512]{1,0:T(8,128)(2,1)}, bf16[256,512]{1,0:T(8,128)(2,1)S(1)}, u32[]{:S(2)}, u32[]{:S(2)}) collective-permute-start(bf16[256,512]{1,0:T(8,128)(2,1)} %keys_and_values.1.kv), channel_id=1, source_target_pairs={{0,64},{8,72},{16,80},{24,88},{32,96},{40,104},{48,112},{56,120},{... | collective-permute-start | bytes 786440 | tf_op jit(solution)/shard_map/ppermute | solution.py:22
  12.1 1.0 %copy-done.2 = bf16[256,1024]{1,0:T(8,128)(2,1)S(1)} copy-done((bf16[256,1024]{1,0:T(8,128)(2,1)S(1)}, bf16[256,1024]{1,0:T(8,128)(2,1)}, u32[]{:S(2)}) %copy-start.2) | copy-done | bytes 524312
  14.2 2.2 %own_block.1 = (f32[1024,256]{1,0:T(8,128)S(1)}, f32[256,512]{1,0:T(8,128)S(1)}, f32[8,256]{1,0:T(8,128)S(1)}, s32[1,256]{1,0:T(1,128)S(1)}) custom-call(s32[1]{0:T(128)} %bitcast.index, s32[16]{0:T(128)S(1)} %copy-done.6, bf16[256,1024]{1,0:T(8,128)(2,1)S(1)} %copy-done.2, bf16[256,1024]{1,0:T(8,128)(2,1)S(1)} %copy-done.4, ...), custom_call_target="tpu_custom_call" | custom-call | flops 671088640 | bytes 3145728 | tf_op jit(solution)/shard_map/own_block/pallas_call | solution.py:173
  16.4 4.2 %collective-permute-start.3 = (bf16[256,512]{1,0:T(8,128)(2,1)S(1)}, bf16[256,512]{1,0:T(8,128)(2,1)S(1)}, u32[]{:S(2)}, u32[]{:S(2)}) collective-permute-start(bf16[256,512]{1,0:T(8,128)(2,1)S(1)} %collective-permute-done.1.kv), channel_id=1, source_target_pairs={{0,8},{8,16},{16,24},{24,32},{32,40},{40,48},{48,56},{56,64},{64,7... | collective-permute-start | bytes 786440 | tf_op jit(solution)/shard_map/ppermute | solution.py:17
  20.7 1.6 %block_1.1 = (f32[1024,256]{1,0:T(8,128)S(1)}, bf16[256,512]{1,0:T(8,128)(2,1)S(1)}) custom-call(s32[1,256]{1,0:T(1,128)S(1)} %get-tuple-element.37.starts, bf16[256,1024]{1,0:T(8,128)(2,1)S(1)} %copy-done.2, bf16[256,1024]{1,0:T(8,128)(2,1)S(1)} %copy-done.4, f32[8,256]{1,0:T(8,128)S(1)} %copy-done.5, ...), custom_call_target="tpu_custom_call", output_to_operand_aliasing={{0}: (6, {})} | custom-call | flops 671088640 | bytes 3145728 | tf_op jit(solution)/shard_map/block_1/pallas_call | solution.py:180
  22.3 1.9 %collective-permute-start.2 = (bf16[256,512]{1,0:T(8,128)(2,1)S(1)}, bf16[256,512]{1,0:T(8,128)(2,1)S(1)}, u32[]{:S(2)}, u32[]{:S(2)}) collective-permute-start(bf16[256,512]{1,0:T(8,128)(2,1)S(1)} %collective-permute-done.kv), channel_id=1, source_target_pairs={{0,504},{8,0},{16,8},{24,16},{32,24},{40,32},{48,40},{56,48},{64,5... | collective-permute-start | bytes 786440 | tf_op jit(solution)/shard_map/ppermute | solution.py:22
  24.4 1.4 %collective-permute-done.3.kv = bf16[256,512]{1,0:T(8,128)(2,1)S(1)} collective-permute-done((bf16[256,512]{1,0:T(8,128)(2,1)S(1)}, bf16[256,512]{1,0:T(8,128)(2,1)S(1)}, u32[]{:S(2)}, u32[]{:S(2)}) %collective-permute-start.3) | collective-permute-done | bytes 262176 | tf_op jit(solution)/shard_map/ppermute | solution.py:17
  25.8 7.2 %collective-permute-start.5 = (bf16[256,512]{1,0:T(8,128)(2,1)S(1)}, bf16[256,512]{1,0:T(8,128)(2,1)S(1)}, u32[]{:S(2)}, u32[]{:S(2)}) collective-permute-start(bf16[256,512]{1,0:T(8,128)(2,1)S(1)} %collective-permute-done.3.kv), channel_id=1, source_target_pairs={{0,8},{8,16},{16,24},{24,32},{32,40},{40,48},{48,56},{56,64},{64,7... | collective-permute-start | bytes 786440 | tf_op jit(solution)/shard_map/ppermute | solution.py:17
  33.0 1.6 %block_2.1 = (f32[1024,256]{1,0:T(8,128)S(1)}, bf16[256,512]{1,0:T(8,128)(2,1)S(1)}) custom-call(s32[1,256]{1,0:T(1,128)S(1)} %get-tuple-element.37.starts, bf16[256,1024]{1,0:T(8,128)(2,1)S(1)} %copy-done.2, bf16[256,1024]{1,0:T(8,128)(2,1)S(1)} %copy-done.4, f32[8,256]{1,0:T(8,128)S(1)} %copy-done.5, ...), custom_call_target="tpu_custom_call", output_to_operand_aliasing={{0}: (6, {})} | custom-call | flops 671088640 | bytes 3145728 | tf_op jit(solution)/shard_map/block_2/pallas_call | solution.py:180
  34.6 2.1 %collective-permute-start.4 = (bf16[256,512]{1,0:T(8,128)(2,1)S(1)}, bf16[256,512]{1,0:T(8,128)(2,1)S(1)}, u32[]{:S(2)}, u32[]{:S(2)}) collective-permute-start(bf16[256,512]{1,0:T(8,128)(2,1)S(1)} %collective-permute-done.2.kv), channel_id=1, source_target_pairs={{0,504},{8,0},{16,8},{24,16},{32,24},{40,32},{48,40},{56,48},{64,5... | collective-permute-start | bytes 786440 | tf_op jit(solution)/shard_map/ppermute | solution.py:22
  36.7 1.6 %block_7.1 = (f32[1024,256]{1,0:T(8,128)S(1)}, bf16[256,512]{1,0:T(8,128)(2,1)S(1)}) custom-call(s32[1,256]{1,0:T(1,128)S(1)} %get-tuple-element.37.starts, bf16[256,1024]{1,0:T(8,128)(2,1)S(1)} %copy-done.2, bf16[256,1024]{1,0:T(8,128)(2,1)S(1)} %copy-done.4, f32[8,256]{1,0:T(8,128)S(1)} %copy-done.5, ...), custom_call_target="tpu_custom_call", output_to_operand_aliasing={{0}: (6, {})} | custom-call | flops 671088640 | bytes 3145728 | tf_op jit(solution)/shard_map/block_7/pallas_call | solution.py:180
  38.3 6.2 %collective-permute-start.7 = (bf16[256,512]{1,0:T(8,128)(2,1)S(1)}, bf16[256,512]{1,0:T(8,128)(2,1)S(1)}, u32[]{:S(2)}, u32[]{:S(2)}) collective-permute-start(bf16[256,512]{1,0:T(8,128)(2,1)S(1)} %collective-permute-done.5.kv), channel_id=1, source_target_pairs={{0,8},{8,16},{16,24},{24,32},{32,40},{40,48},{48,56},{56,64},{64,7... | collective-permute-start | bytes 786440 | tf_op jit(solution)/shard_map/ppermute | solution.py:17
  44.6 1.6 %block_3.1 = (f32[1024,256]{1,0:T(8,128)S(1)}, bf16[256,512]{1,0:T(8,128)(2,1)S(1)}) custom-call(s32[1,256]{1,0:T(1,128)S(1)} %get-tuple-element.37.starts, bf16[256,1024]{1,0:T(8,128)(2,1)S(1)} %copy-done.3, bf16[256,1024]{1,0:T(8,128)(2,1)S(1)} %copy-done.4, f32[8,256]{1,0:T(8,128)S(1)} %copy-done.5, ...), custom_call_target="tpu_custom_call", output_to_operand_aliasing={{0}: (6, {})} | custom-call | flops 671088640 | bytes 3145728 | tf_op jit(solution)/shard_map/block_3/pallas_call | solution.py:180
  46.3 1.9 %collective-permute-start.6 = (bf16[256,512]{1,0:T(8,128)(2,1)S(1)}, bf16[256,512]{1,0:T(8,128)(2,1)S(1)}, u32[]{:S(2)}, u32[]{:S(2)}) collective-permute-start(bf16[256,512]{1,0:T(8,128)(2,1)S(1)} %collective-permute-done.4.kv), channel_id=1, source_target_pairs={{0,504},{8,0},{16,8},{24,16},{32,24},{40,32},{48,40},{56,48},{64,5... | collective-permute-start | bytes 786440 | tf_op jit(solution)/shard_map/ppermute | solution.py:22
  48.4 1.8 %block_4.1 = (f32[1024,256]{1,0:T(8,128)S(1)}, bf16[256,512]{1,0:T(8,128)(2,1)S(1)}) custom-call(s32[1,256]{1,0:T(1,128)S(1)} %get-tuple-element.37.starts, bf16[256,1024]{1,0:T(8,128)(2,1)S(1)} %copy-done.3, bf16[256,1024]{1,0:T(8,128)(2,1)S(1)} %copy-done.4, f32[8,256]{1,0:T(8,128)S(1)} %copy-done.5, ...), custom_call_target="tpu_custom_call", output_to_operand_aliasing={{0}: (6, {})} | custom-call | flops 671088640 | bytes 3145728 | tf_op jit(solution)/shard_map/block_4/pallas_call | solution.py:180
  50.2 1.9 %collective-permute-start.12 = (bf16[256,512]{1,0:T(8,128)(2,1)S(1)}, bf16[256,512]{1,0:T(8,128)(2,1)S(1)}, u32[]{:S(2)}, u32[]{:S(2)}) collective-permute-start(bf16[256,512]{1,0:T(8,128)(2,1)S(1)} %get-tuple-element.65), channel_id=1, source_target_pairs={{8,0},{16,8},{24,16},{32,24},{40,32},{48,40},{56,48},{64,56},{72,6... | collective-permute-start | bytes 786440 | tf_op jit(solution)/shard_map/ppermute | solution.py:17
  52.2 1.6 %block_6.1 = (f32[1024,256]{1,0:T(8,128)S(1)}, bf16[256,512]{1,0:T(8,128)(2,1)S(1)}) custom-call(s32[1,256]{1,0:T(1,128)S(1)} %get-tuple-element.37.starts, bf16[256,1024]{1,0:T(8,128)(2,1)S(1)} %copy-done.3, bf16[256,1024]{1,0:T(8,128)(2,1)S(1)} %copy-done.4, f32[8,256]{1,0:T(8,128)S(1)} %copy-done.5, ...), custom_call_target="tpu_custom_call", output_to_operand_aliasing={{0}: (6, {})} | custom-call | flops 671088640 | bytes 3145728 | tf_op jit(solution)/shard_map/block_6/pallas_call | solution.py:180
  53.8 6.3 %collective-permute-done.6.kv = bf16[256,512]{1,0:T(8,128)(2,1)S(1)} collective-permute-done((bf16[256,512]{1,0:T(8,128)(2,1)S(1)}, bf16[256,512]{1,0:T(8,128)(2,1)S(1)}, u32[]{:S(2)}, u32[]{:S(2)}) %collective-permute-start.6) | collective-permute-done | bytes 262176 | tf_op jit(solution)/shard_map/ppermute | solution.py:22
  60.1 1.6 %block_5.1 = (f32[1024,256]{1,0:T(8,128)S(1)}, bf16[256,512]{1,0:T(8,128)(2,1)S(1)}) custom-call(s32[1,256]{1,0:T(1,128)S(1)} %get-tuple-element.37.starts, bf16[256,1024]{1,0:T(8,128)(2,1)S(1)} %copy-done.3, bf16[256,1024]{1,0:T(8,128)(2,1)S(1)} %copy-done.4, f32[8,256]{1,0:T(8,128)S(1)} %copy-done.5, ...), custom_call_target="tpu_custom_call", output_to_operand_aliasing={{0}: (6, {})} | custom-call | flops 671088640 | bytes 3145728 | tf_op jit(solution)/shard_map/block_5/pallas_call | solution.py:180
  61.8 1.9 %collective-permute-start.8 = (bf16[256,512]{1,0:T(8,128)(2,1)S(1)}, bf16[256,512]{1,0:T(8,128)(2,1)S(1)}, u32[]{:S(2)}, u32[]{:S(2)}) collective-permute-start(bf16[256,512]{1,0:T(8,128)(2,1)S(1)} %get-tuple-element.61), channel_id=1, source_target_pairs={{0,16},{8,24},{16,32},{24,40},{32,48},{40,56},{48,64},{56,72},{64,... | collective-permute-start | bytes 786440 | tf_op jit(solution)/shard_map/ppermute | solution.py:22
  63.7 1.9 %collective-permute-start.9 = (bf16[256,512]{1,0:T(8,128)(2,1)S(1)}, bf16[256,512]{1,0:T(8,128)(2,1)S(1)}, u32[]{:S(2)}, u32[]{:S(2)}) collective-permute-start(bf16[256,512]{1,0:T(8,128)(2,1)S(1)} %get-tuple-element.62), channel_id=1, source_target_pairs={{0,8},{8,16},{16,24},{24,32},{32,40},{40,48},{48,56},{56,64},{64,7... | collective-permute-start | bytes 786440 | tf_op jit(solution)/shard_map/ppermute | solution.py:22
  65.6 3.9 %collective-permute-start.14 = (bf16[256,512]{1,0:T(8,128)(2,1)S(1)}, bf16[256,512]{1,0:T(8,128)(2,1)S(1)}, u32[]{:S(2)}, u32[]{:S(2)}) collective-permute-start(bf16[256,512]{1,0:T(8,128)(2,1)S(1)} %get-tuple-element.67), channel_id=1, source_target_pairs={{8,0},{16,8},{24,16},{32,24},{40,32},{48,40},{56,48},{64,56},{72,6... | collective-permute-start | bytes 786440 | tf_op jit(solution)/shard_map/ppermute | solution.py:17
  69.6 4.8 %collective-permute-start.13 = (bf16[256,512]{1,0:T(8,128)(2,1)S(1)}, bf16[256,512]{1,0:T(8,128)(2,1)S(1)}, u32[]{:S(2)}, u32[]{:S(2)}) collective-permute-start(bf16[256,512]{1,0:T(8,128)(2,1)S(1)} %add_convert_fusion.1), channel_id=1, source_target_pairs={{16,0},{24,8},{32,16},{40,24},{48,32},{56,40},{64,48},{72,56},{80,... | collective-permute-start | bytes 786440 | tf_op jit(solution)/shard_map/ppermute | solution.py:17
  74.4 1.9 %collective-permute-start.11 = (bf16[256,512]{1,0:T(8,128)(2,1)S(1)}, bf16[256,512]{1,0:T(8,128)(2,1)S(1)}, u32[]{:S(2)}, u32[]{:S(2)}) collective-permute-start(bf16[256,512]{1,0:T(8,128)(2,1)S(1)} %get-tuple-element.64), channel_id=1, source_target_pairs={{64,0},{72,8},{80,16},{88,24},{96,32},{104,40},{112,48},{120,56},{... | collective-permute-start | bytes 786440 | tf_op jit(solution)/shard_map/ppermute | solution.py:17
  76.6 1.9 %collective-permute-start.10 = (bf16[256,512]{1,0:T(8,128)(2,1)S(1)}, bf16[256,512]{1,0:T(8,128)(2,1)S(1)}, u32[]{:S(2)}, u32[]{:S(2)}) collective-permute-start(bf16[256,512]{1,0:T(8,128)(2,1)S(1)} %add_convert_fusion.2), channel_id=1, source_target_pairs={{0,456},{8,464},{16,472},{24,480},{32,488},{40,496},{48,504},{56,0... | collective-permute-start | bytes 786440 | tf_op jit(solution)/shard_map/ppermute | solution.py:22
  78.6 6.0 %collective-permute-done.14 = bf16[256,512]{1,0:T(8,128)(2,1)S(1)} collective-permute-done((bf16[256,512]{1,0:T(8,128)(2,1)S(1)}, bf16[256,512]{1,0:T(8,128)(2,1)S(1)}, u32[]{:S(2)}, u32[]{:S(2)}) %collective-permute-start.14) | collective-permute-done | bytes 262176 | tf_op jit(solution)/shard_map/ppermute | solution.py:17
  84.6 2.7 %collective-permute-done.13 = bf16[256,512]{1,0:T(8,128)(2,1)S(1)} collective-permute-done((bf16[256,512]{1,0:T(8,128)(2,1)S(1)}, bf16[256,512]{1,0:T(8,128)(2,1)S(1)}, u32[]{:S(2)}, u32[]{:S(2)}) %collective-permute-start.13) | collective-permute-done | bytes 262176 | tf_op jit(solution)/shard_map/ppermute | solution.py:17
  87.4 6.2 %collective-permute-start.15 = (bf16[256,512]{1,0:T(8,128)(2,1)S(1)}, bf16[256,512]{1,0:T(8,128)(2,1)S(1)}, u32[]{:S(2)}, u32[]{:S(2)}) collective-permute-start(bf16[256,512]{1,0:T(8,128)(2,1)S(1)} %add_convert_fusion), channel_id=1, source_target_pairs={{8,0},{16,8},{24,16},{32,24},{40,32},{48,40},{56,48},{64,56},{72,6... | collective-permute-start | bytes 786440 | tf_op jit(solution)/shard_map/ppermute | solution.py:17
  93.6 1.1 %turn_query_gradient.1 = bf16[256,1024]{1,0:T(8,128)(2,1)} custom-call(f32[1024,256]{1,0:T(8,128)S(1)} %get-tuple-element.59.dq_t), custom_call_target="tpu_custom_call" | custom-call | bytes 3145728 | tf_op jit(solution)/shard_map/turn_query_gradient/pallas_call | solution.py:212
  94.7 4.2 %collective-permute-done.15.refs_2_ = bf16[256,512]{1,0:T(8,128)(2,1)S(1)} collective-permute-done((bf16[256,512]{1,0:T(8,128)(2,1)S(1)}, bf16[256,512]{1,0:T(8,128)(2,1)S(1)}, u32[]{:S(2)}, u32[]{:S(2)}) %collective-permute-start.15) | collective-permute-done | bytes 262176 | tf_op jit(solution)/shard_map/ppermute | solution.py:17
  (29 shorter events, 4.4 us)
Async XLA Ops:
  0.6 9.9 %copy-start.1 = (bf16[256,1024]{1,0:T(8,128)(2,1)S(1)}, bf16[256,1024]{1,0:T(8,128)(2,1)}, u32[]{:S(2)}) copy-start(bf16[256,1024]{1,0:T(8,128)(2,1)} %o.1) | copy-start | bytes 1572868
  2.4 8.1 %copy-start.5 = (f32[8,256]{1,0:T(8,128)S(1)}, f32[8,256]{1,0:T(8,128)}, u32[]{:S(2)}) copy-start(f32[8,256]{1,0:T(8,128)} %lse.17) | copy-start | bytes 24580
  2.4 14.0 %collective-permute-start.1 = (bf16[256,512]{1,0:T(8,128)(2,1)}, bf16[256,512]{1,0:T(8,128)(2,1)S(1)}, u32[]{:S(2)}, u32[]{:S(2)}) collective-permute-start(bf16[256,512]{1,0:T(8,128)(2,1)} %keys_and_values.1.kv), channel_id=1, source_target_pairs={{0,8},{8,16},{16,24},{24,32},{32,40},{40,48},{48,56},{56,64},{64,7... | collective-permute-start | bytes 786440 | tf_op jit(solution)/shard_map/ppermute | solution.py:17
  7.1 15.2 %collective-permute-start = (bf16[256,512]{1,0:T(8,128)(2,1)}, bf16[256,512]{1,0:T(8,128)(2,1)S(1)}, u32[]{:S(2)}, u32[]{:S(2)}) collective-permute-start(bf16[256,512]{1,0:T(8,128)(2,1)} %keys_and_values.1.kv), channel_id=1, source_target_pairs={{0,64},{8,72},{16,80},{24,88},{32,96},{40,104},{48,112},{56,120},{... | collective-permute-start | bytes 786440 | tf_op jit(solution)/shard_map/ppermute | solution.py:22
  10.5 0.7 copy-start.6
  11.2 0.9 copy-start
  12.1 1.0 %copy-start.2 = (bf16[256,1024]{1,0:T(8,128)(2,1)S(1)}, bf16[256,1024]{1,0:T(8,128)(2,1)}, u32[]{:S(2)}) copy-start(bf16[256,1024]{1,0:T(8,128)(2,1)} %q.17) | copy-start | bytes 1572868
  13.2 1.0 %copy-start.4 = (bf16[256,1024]{1,0:T(8,128)(2,1)S(1)}, bf16[256,1024]{1,0:T(8,128)(2,1)}, u32[]{:S(2)}) copy-start(bf16[256,1024]{1,0:T(8,128)(2,1)} %do.17) | copy-start | bytes 1572868
  16.4 9.4 %collective-permute-start.3 = (bf16[256,512]{1,0:T(8,128)(2,1)S(1)}, bf16[256,512]{1,0:T(8,128)(2,1)S(1)}, u32[]{:S(2)}, u32[]{:S(2)}) collective-permute-start(bf16[256,512]{1,0:T(8,128)(2,1)S(1)} %collective-permute-done.1.kv), channel_id=1, source_target_pairs={{0,8},{8,16},{16,24},{24,32},{32,40},{40,48},{48,56},{56,64},{64,7... | collective-permute-start | bytes 786440 | tf_op jit(solution)/shard_map/ppermute | solution.py:17
  22.3 12.3 %collective-permute-start.2 = (bf16[256,512]{1,0:T(8,128)(2,1)S(1)}, bf16[256,512]{1,0:T(8,128)(2,1)S(1)}, u32[]{:S(2)}, u32[]{:S(2)}) collective-permute-start(bf16[256,512]{1,0:T(8,128)(2,1)S(1)} %collective-permute-done.kv), channel_id=1, source_target_pairs={{0,504},{8,0},{16,8},{24,16},{32,24},{40,32},{48,40},{56,48},{64,5... | collective-permute-start | bytes 786440 | tf_op jit(solution)/shard_map/ppermute | solution.py:22
  25.8 12.5 %collective-permute-start.5 = (bf16[256,512]{1,0:T(8,128)(2,1)S(1)}, bf16[256,512]{1,0:T(8,128)(2,1)S(1)}, u32[]{:S(2)}, u32[]{:S(2)}) collective-permute-start(bf16[256,512]{1,0:T(8,128)(2,1)S(1)} %collective-permute-done.3.kv), channel_id=1, source_target_pairs={{0,8},{8,16},{16,24},{24,32},{32,40},{40,48},{48,56},{56,64},{64,7... | collective-permute-start | bytes 786440 | tf_op jit(solution)/shard_map/ppermute | solution.py:17
  34.6 10.0 %copy-start.3 = (bf16[256,1024]{1,0:T(8,128)(2,1)S(1)}, bf16[256,1024]{1,0:T(8,128)(2,1)}, u32[]{:S(2)}) copy-start(bf16[256,1024]{1,0:T(8,128)(2,1)} %q.17) | copy-start | bytes 1572868
  34.6 11.7 %collective-permute-start.4 = (bf16[256,512]{1,0:T(8,128)(2,1)S(1)}, bf16[256,512]{1,0:T(8,128)(2,1)S(1)}, u32[]{:S(2)}, u32[]{:S(2)}) collective-permute-start(bf16[256,512]{1,0:T(8,128)(2,1)S(1)} %collective-permute-done.2.kv), channel_id=1, source_target_pairs={{0,504},{8,0},{16,8},{24,16},{32,24},{40,32},{48,40},{56,48},{64,5... | collective-permute-start | bytes 786440 | tf_op jit(solution)/shard_map/ppermute | solution.py:22
  38.3 10.1 %collective-permute-start.7 = (bf16[256,512]{1,0:T(8,128)(2,1)S(1)}, bf16[256,512]{1,0:T(8,128)(2,1)S(1)}, u32[]{:S(2)}, u32[]{:S(2)}) collective-permute-start(bf16[256,512]{1,0:T(8,128)(2,1)S(1)} %collective-permute-done.5.kv), channel_id=1, source_target_pairs={{0,8},{8,16},{16,24},{24,32},{32,40},{40,48},{48,56},{56,64},{64,7... | collective-permute-start | bytes 786440 | tf_op jit(solution)/shard_map/ppermute | solution.py:17
  46.3 13.8 %collective-permute-start.6 = (bf16[256,512]{1,0:T(8,128)(2,1)S(1)}, bf16[256,512]{1,0:T(8,128)(2,1)S(1)}, u32[]{:S(2)}, u32[]{:S(2)}) collective-permute-start(bf16[256,512]{1,0:T(8,128)(2,1)S(1)} %collective-permute-done.4.kv), channel_id=1, source_target_pairs={{0,504},{8,0},{16,8},{24,16},{32,24},{40,32},{48,40},{56,48},{64,5... | collective-permute-start | bytes 786440 | tf_op jit(solution)/shard_map/ppermute | solution.py:22
  50.2 19.3 %collective-permute-start.12 = (bf16[256,512]{1,0:T(8,128)(2,1)S(1)}, bf16[256,512]{1,0:T(8,128)(2,1)S(1)}, u32[]{:S(2)}, u32[]{:S(2)}) collective-permute-start(bf16[256,512]{1,0:T(8,128)(2,1)S(1)} %get-tuple-element.65), channel_id=1, source_target_pairs={{8,0},{16,8},{24,16},{32,24},{40,32},{48,40},{56,48},{64,56},{72,6... | collective-permute-start | bytes 786440 | tf_op jit(solution)/shard_map/ppermute | solution.py:17
  61.8 14.6 %collective-permute-start.8 = (bf16[256,512]{1,0:T(8,128)(2,1)S(1)}, bf16[256,512]{1,0:T(8,128)(2,1)S(1)}, u32[]{:S(2)}, u32[]{:S(2)}) collective-permute-start(bf16[256,512]{1,0:T(8,128)(2,1)S(1)} %get-tuple-element.61), channel_id=1, source_target_pairs={{0,16},{8,24},{16,32},{24,40},{32,48},{40,56},{48,64},{56,72},{64,... | collective-permute-start | bytes 786440 | tf_op jit(solution)/shard_map/ppermute | solution.py:22
  63.7 12.8 %collective-permute-start.9 = (bf16[256,512]{1,0:T(8,128)(2,1)S(1)}, bf16[256,512]{1,0:T(8,128)(2,1)S(1)}, u32[]{:S(2)}, u32[]{:S(2)}) collective-permute-start(bf16[256,512]{1,0:T(8,128)(2,1)S(1)} %get-tuple-element.62), channel_id=1, source_target_pairs={{0,8},{8,16},{16,24},{24,32},{32,40},{40,48},{48,56},{56,64},{64,7... | collective-permute-start | bytes 786440 | tf_op jit(solution)/shard_map/ppermute | solution.py:22
  65.6 19.0 %collective-permute-start.14 = (bf16[256,512]{1,0:T(8,128)(2,1)S(1)}, bf16[256,512]{1,0:T(8,128)(2,1)S(1)}, u32[]{:S(2)}, u32[]{:S(2)}) collective-permute-start(bf16[256,512]{1,0:T(8,128)(2,1)S(1)} %get-tuple-element.67), channel_id=1, source_target_pairs={{8,0},{16,8},{24,16},{32,24},{40,32},{48,40},{56,48},{64,56},{72,6... | collective-permute-start | bytes 786440 | tf_op jit(solution)/shard_map/ppermute | solution.py:17
  69.6 17.7 %collective-permute-start.13 = (bf16[256,512]{1,0:T(8,128)(2,1)S(1)}, bf16[256,512]{1,0:T(8,128)(2,1)S(1)}, u32[]{:S(2)}, u32[]{:S(2)}) collective-permute-start(bf16[256,512]{1,0:T(8,128)(2,1)S(1)} %add_convert_fusion.1), channel_id=1, source_target_pairs={{16,0},{24,8},{32,16},{40,24},{48,32},{56,40},{64,48},{72,56},{80,... | collective-permute-start | bytes 786440 | tf_op jit(solution)/shard_map/ppermute | solution.py:17
  74.4 20.3 %collective-permute-start.11 = (bf16[256,512]{1,0:T(8,128)(2,1)S(1)}, bf16[256,512]{1,0:T(8,128)(2,1)S(1)}, u32[]{:S(2)}, u32[]{:S(2)}) collective-permute-start(bf16[256,512]{1,0:T(8,128)(2,1)S(1)} %get-tuple-element.64), channel_id=1, source_target_pairs={{64,0},{72,8},{80,16},{88,24},{96,32},{104,40},{112,48},{120,56},{... | collective-permute-start | bytes 786440 | tf_op jit(solution)/shard_map/ppermute | solution.py:17
  76.6 18.1 %collective-permute-start.10 = (bf16[256,512]{1,0:T(8,128)(2,1)S(1)}, bf16[256,512]{1,0:T(8,128)(2,1)S(1)}, u32[]{:S(2)}, u32[]{:S(2)}) collective-permute-start(bf16[256,512]{1,0:T(8,128)(2,1)S(1)} %add_convert_fusion.2), channel_id=1, source_target_pairs={{0,456},{8,464},{16,472},{24,480},{32,488},{40,496},{48,504},{56,0... | collective-permute-start | bytes 786440 | tf_op jit(solution)/shard_map/ppermute | solution.py:22
  87.4 11.6 %collective-permute-start.15 = (bf16[256,512]{1,0:T(8,128)(2,1)S(1)}, bf16[256,512]{1,0:T(8,128)(2,1)S(1)}, u32[]{:S(2)}, u32[]{:S(2)}) collective-permute-start(bf16[256,512]{1,0:T(8,128)(2,1)S(1)} %add_convert_fusion), channel_id=1, source_target_pairs={{8,0},{16,8},{24,16},{32,24},{40,32},{48,40},{56,48},{64,56},{72,6... | collective-permute-start | bytes 786440 | tf_op jit(solution)/shard_map/ppermute | solution.py:17
